TPU v7x, 32 devices: a whole 2x2x4 slice. The times are simulated.
32 devices in a mesh: dp: 4 (over x, core), expert: 8 (over z, y).
Axes of the slice: x: 2, y: 2, z: 4, core: 2. Of those that a mesh axis runs over, the one named last changes fastest.
Arguments:
- tokens: bfloat16 [8192, 1024], P(('dp', 'expert')), may hold values from -6 to 6
- norm_gain: float32 [1024], replicated, may hold values from 0.5 to 1.5
- query_weight: bfloat16 [1024, 512], replicated, may hold values from -0.1875 to 0.1875
- key_weight: bfloat16 [1024, 512], replicated, may hold values from -0.1875 to 0.1875
- value_weight: bfloat16 [1024, 2560], replicated, may hold values from -0.1875 to 0.1875
- output_weight: bfloat16 [1024, 2560], replicated, may hold values from -3 to 3
- value_router: bfloat16 [1024, 20], replicated, may hold values from -0.125 to 0.125
- output_router: bfloat16 [1024, 20], replicated, may hold values from -0.125 to 0.125
- expert_router: bfloat16 [1024, 192], replicated, may hold values from -0.0625 to 0.0625
- expert_up: bfloat16 [192, 1024, 128], P('expert'), may hold values from -0.125 to 0.125
- expert_down: bfloat16 [192, 1024, 128], P('expert'), may hold values from -0.5 to 0.5
- lengths: int32 [32], P(('dp', 'expert')), may hold values from 64 to 256, as said below
- value_choice: int32 [8192, 4, 2], P(('dp', 'expert')), may hold values from 0 to 4, all different within a row
- output_choice: int32 [8192, 4, 2], P(('dp', 'expert')), may hold values from 0 to 4, all different within a row
- expert_choice: int32 [8192, 16], P(('dp', 'expert')), may hold values from 0 to 191, all different within a row; in each aligned block of 256 rows (0 to 255, 256 to 511, ...) at most 32 rows name the same one
- running_counts: int32 [192], P(('dp', 'expert')), may hold values from 0 to 63
- cotangent: bfloat16 [8192, 1024], P(('dp', 'expert')), may hold values from -6 to 6
Outputs:
- output: bfloat16 [8192, 1024], P(('dp', 'expert'))
- grad_tokens: bfloat16 [8192, 1024], P(('dp', 'expert'))
- grad_gain: float32 [1024], P(('dp', 'expert'))
- grad_query: float32 [1024, 512], P(('dp', 'expert'))
- grad_key: float32 [1024, 512], P(('dp', 'expert'))
- grad_value: float32 [1024, 2560], P(('dp', 'expert'))
- grad_output: float32 [1024, 2560], P(('dp', 'expert'))
- grad_value_router: float32 [1024, 20], P(('dp', 'expert'))
- grad_output_router: float32 [1024, 20], P(('dp', 'expert'))
- grad_expert_router: float32 [1024, 192], P(('dp', 'expert'))
- grad_expert_up: float32 [192, 1024, 128], P('expert', 'dp')
- grad_expert_down: float32 [192, 1024, 128], P('expert', 'dp')
- counts: int32 [192], P(('dp', 'expert'))
Inputs may be any that keep to these rules, and one draw needn't show every extreme that they name: `lengths`: some sequence has length exactly 256. `value_choice`: A token names 2 different experts in each head. `output_choice`: A token names 2 different experts in each head. `expert_choice`: A token names 16 different experts; within the 256 rows of one device no expert is named more than 32 times, a bound that some block reaches there.
All inputs are finite; a program needn't handle non-finite values.
Results may differ from a plain program's by a relative error of at most 0.012.
The roundings to bfloat16 on the way count: a program that leaves them out, or rounds other values in their place, can miss the bound.
Values may be sent and summed in bfloat16 or wider, within the bound.
No kernel may reach another device: no remote copies, remote signals or barrier semaphores. Data moves between devices by JAX's collectives and lax.ppermute only.
A program may use at most 256 MiB of HBM per device.

v0:
```python
import math

import jax
import jax.numpy as jnp
from jax import lax
from jax.sharding import PartitionSpec as P

HEADS = 4
HEAD = 128
AEXP = 5


def rope_tables(seq_rows, head_width):
    half_width = head_width // 2
    ladder = jnp.arange(half_width, dtype=jnp.float32) * (2.0 / head_width)
    freqs = jnp.exp(-math.log(10000.0) * ladder)
    angles = jnp.arange(seq_rows, dtype=jnp.float32)[:, None] * freqs[None, :]
    return (jnp.cos(angles), jnp.sin(angles))


def rotate(vectors, cosine, sine):
    half_width = vectors.shape[-1] // 2
    former = vectors[..., :half_width]
    latter = vectors[..., half_width:]
    cos_rows = cosine[:, None, :]
    sin_rows = sine[:, None, :]
    return jnp.concatenate(
        [former * cos_rows - latter * sin_rows, former * sin_rows + latter * cos_rows], axis=-1
    )


def unrotate(grads, cosine, sine):
    half_width = grads.shape[-1] // 2
    former = grads[..., :half_width]
    latter = grads[..., half_width:]
    cos_rows = cosine[:, None, :]
    sin_rows = sine[:, None, :]
    return jnp.concatenate(
        [former * cos_rows + latter * sin_rows, latter * cos_rows - former * sin_rows], axis=-1
    )


def slots(picks, experts_all, capacity):
    seq_rows, picks_per = picks.shape
    labels = jnp.arange(experts_all, dtype=jnp.int32)
    member = jnp.sum(
        (picks[:, :, None] == labels[None, None, :]).astype(jnp.int32), axis=1, dtype=jnp.int32
    )
    earlier = jnp.cumsum(member, axis=0, dtype=jnp.int32) - member
    places = jnp.take_along_axis(earlier, picks, axis=1)
    flat = picks * capacity + places
    filler = jnp.full((experts_all * capacity,), seq_rows * picks_per, jnp.int32)
    owner = filler.at[flat.reshape(-1)].set(jnp.arange(seq_rows * picks_per, dtype=jnp.int32))
    return (member, flat, owner)


def block_scores(query_blk, key_rot, start, seq_length, score_scale):
    block_rows = query_blk.shape[0]
    query_pos = start + jnp.arange(block_rows, dtype=jnp.int32)
    key_pos = jnp.arange(key_rot.shape[0], dtype=jnp.int32)
    allowed = (key_pos[None, :] <= query_pos[:, None]) & (key_pos[None, :] < seq_length)
    scores = (
        jnp.einsum("qhw,khw->hqk", query_blk, key_rot, preferred_element_type=jnp.float32)
        * score_scale
    )
    return jnp.where(allowed[None], scores, -1e30)


def contract_rows(left, right):
    return lax.dot_general(
        left, right, (((0,), (0,)), ((), ())), preferred_element_type=jnp.float32
    )


def contract_cols(left, right):
    return lax.dot_general(
        left, right, (((1,), (1,)), ((), ())), preferred_element_type=jnp.float32
    )


def expert_forward(received, expert_up, expert_down):
    pre = jnp.einsum("sjcd,jdf->sjcf", received, expert_up, preferred_element_type=jnp.float32)
    act = jax.nn.gelu(pre).astype(jnp.bfloat16)
    expert_rows = jnp.einsum(
        "sjcf,jdf->sjcd", act, expert_down, preferred_element_type=jnp.float32
    ).astype(jnp.bfloat16)
    return (pre, act, expert_rows)


def expert_backward(received, pre, act, grad_recv, expert_up, expert_down):
    dact = jnp.einsum("sjcd,jdf->sjcf", grad_recv, expert_down, preferred_element_type=jnp.float32)
    gelu_value, gelu_pull = jax.vjp(jax.nn.gelu, pre)
    dpre_low = gelu_pull(dact)[0].astype(jnp.bfloat16)
    grad_down = jnp.einsum("sjcd,sjcf->jdf", grad_recv, act, preferred_element_type=jnp.float32)
    grad_up = jnp.einsum("sjcd,sjcf->jdf", received, dpre_low, preferred_element_type=jnp.float32)
    drows_expert = jnp.einsum(
        "sjcf,jdf->sjcd", dpre_low, expert_up, preferred_element_type=jnp.float32
    ).astype(jnp.bfloat16)
    return (grad_up, grad_down, drows_expert)


def shards(
    tokens,
    norm_gain,
    query_weight,
    key_weight,
    value_weight,
    output_weight,
    value_router,
    output_router,
    expert_router,
    expert_up,
    expert_down,
    lengths,
    value_choice,
    output_choice,
    expert_choice,
    running_counts,
    cotangent,
):
    seq_rows, model_width = tokens.shape
    groups = lax.axis_size("expert")
    local_experts = expert_up.shape[0]
    experts_all = local_experts * groups
    picks_per = expert_choice.shape[1]
    capacity = 3 * seq_rows * picks_per // (2 * experts_all)
    block_rows = min(512, seq_rows)
    block_count = seq_rows // block_rows
    score_scale = 1.0 / math.sqrt(HEAD)
    position = jnp.arange(seq_rows, dtype=jnp.int32)
    seq_length = lengths[0]
    valid_int = (position < seq_length).astype(jnp.int32)
    valid_rows = valid_int.astype(jnp.float32)
    inputs = tokens.astype(jnp.float32)
    row_mean = jnp.mean(inputs, axis=1, keepdims=True)
    centered = inputs - row_mean
    inverse_std = lax.rsqrt(jnp.mean(centered * centered, axis=1, keepdims=True) + 1e-05)
    scaled = centered * inverse_std
    normed_low = (scaled * norm_gain).astype(jnp.bfloat16)
    cosine, sine = rope_tables(seq_rows, HEAD)
    query_pre = jnp.dot(normed_low, query_weight, preferred_element_type=jnp.float32).reshape(
        seq_rows, HEADS, HEAD
    )
    key_pre = jnp.dot(normed_low, key_weight, preferred_element_type=jnp.float32).reshape(
        seq_rows, HEADS, HEAD
    )
    query_rot = rotate(query_pre, cosine, sine).astype(jnp.bfloat16)
    key_rot = rotate(key_pre, cosine, sine).astype(jnp.bfloat16)
    values_all = jnp.dot(tokens, value_weight, preferred_element_type=jnp.float32).reshape(
        seq_rows, HEADS, AEXP, HEAD
    )
    labels = jnp.arange(AEXP, dtype=jnp.int32)
    value_mask = jnp.sum((value_choice[..., None] == labels).astype(jnp.float32), axis=2)
    output_mask = jnp.sum((output_choice[..., None] == labels).astype(jnp.float32), axis=2)
    value_sig = jax.nn.sigmoid(
        jnp.dot(tokens, value_router, preferred_element_type=jnp.float32).reshape(
            seq_rows, HEADS, AEXP
        )
    )
    output_sig = jax.nn.sigmoid(
        jnp.dot(tokens, output_router, preferred_element_type=jnp.float32).reshape(
            seq_rows, HEADS, AEXP
        )
    )
    value_gate = value_sig * value_mask
    output_gate = output_sig * output_mask
    mixed = jnp.sum(value_gate[..., None] * values_all, axis=2).astype(jnp.bfloat16)

    def forward_block(index):
        start = index * block_rows
        scores = block_scores(query_rot, key_rot, start, seq_length, score_scale)
        top = jnp.max(scores, axis=2, keepdims=True)
        expo = jnp.exp(scores - top)
        total = jnp.sum(expo, axis=2, keepdims=True)
        probs_low = (expo / total).astype(jnp.bfloat16)
        attended_blk = jnp.einsum(
            "hqk,khw->qhw", probs_low, mixed, preferred_element_type=jnp.float32
        )
        return (attended_blk, (top + jnp.log(total))[:, :, 0])

    attended_blocks, lse_blocks = lax.map(forward_block, jnp.arange(block_count, dtype=jnp.int32))
    attended = attended_blocks.reshape(seq_rows, HEADS, HEAD)
    expanded = (
        (output_gate[..., None] * attended[:, :, None, :])
        .astype(jnp.bfloat16)
        .reshape(seq_rows, HEADS * AEXP * HEAD)
    )
    branch = contract_cols(expanded, output_weight)
    hidden = inputs + branch
    hidden_low = hidden.astype(jnp.bfloat16)
    router_sig = jax.nn.sigmoid(
        jnp.dot(hidden_low, expert_router, preferred_element_type=jnp.float32)
    )
    chosen = jnp.take_along_axis(router_sig, expert_choice, axis=1) * valid_rows[:, None]
    member, flat, owner = slots(expert_choice, experts_all, capacity)
    padded = jnp.concatenate([hidden_low, jnp.zeros((1, model_width), jnp.bfloat16)], axis=0)
    send_rows = padded[owner // picks_per].reshape(groups, local_experts, capacity, model_width)
    grad_out = cotangent.astype(jnp.float32)
    drows_pair = (
        (chosen[:, :, None] * grad_out[:, None, :]).astype(jnp.bfloat16).reshape(-1, model_width)
    )
    dpadded = jnp.concatenate([drows_pair, jnp.zeros((1, model_width), jnp.bfloat16)], axis=0)
    grad_send = dpadded[owner].reshape(groups, local_experts, capacity, model_width)
    received = lax.all_to_all(send_rows, "expert", split_axis=0, concat_axis=0, tiled=True)
    pre, act, expert_rows = expert_forward(received, expert_up, expert_down)
    returned = lax.all_to_all(expert_rows, "expert", split_axis=0, concat_axis=0, tiled=True)
    grad_recv = lax.all_to_all(grad_send, "expert", split_axis=0, concat_axis=0, tiled=True)
    grad_up, grad_down, drows_expert = expert_backward(
        received, pre, act, grad_recv, expert_up, expert_down
    )
    drows_back = lax.all_to_all(drows_expert, "expert", split_axis=0, concat_axis=0, tiled=True)
    back = returned.reshape(-1, model_width)[flat]
    moe = jnp.einsum("tk,tkd->td", chosen, back, preferred_element_type=jnp.float32)
    output = (hidden + moe).astype(jnp.bfloat16)
    dchosen = jnp.einsum("td,tkd->tk", grad_out, back, preferred_element_type=jnp.float32)
    pick_mask = expert_choice[:, :, None] == jnp.arange(experts_all, dtype=jnp.int32)[None, None, :]
    dgate_full = jnp.sum(
        jnp.where(pick_mask, (dchosen * valid_rows[:, None])[:, :, None], 0.0), axis=1
    )
    drouter_low = (dgate_full * router_sig * (1.0 - router_sig)).astype(jnp.bfloat16)
    dhidden_moe = jnp.sum(drows_back.reshape(-1, model_width)[flat], axis=1, dtype=jnp.float32)
    dhidden = grad_out + dhidden_moe + contract_cols(drouter_low, expert_router)
    grad_router = contract_rows(hidden_low, drouter_low)
    dbranch_low = dhidden.astype(jnp.bfloat16)
    grad_output = contract_rows(dbranch_low, expanded)
    dexpanded = jnp.dot(dbranch_low, output_weight, preferred_element_type=jnp.float32).reshape(
        seq_rows, HEADS, AEXP, HEAD
    )
    dattended_low = jnp.sum(output_gate[..., None] * dexpanded, axis=2).astype(jnp.bfloat16)
    doutput_gate = jnp.sum(dexpanded * attended[:, :, None, :], axis=3)
    doutput_logit = (
        (doutput_gate * output_mask * output_sig * (1.0 - output_sig))
        .astype(jnp.bfloat16)
        .reshape(seq_rows, HEADS * AEXP)
    )

    def backward_block(carry, index):
        dkey_total, dmixed_total = carry
        start = index * block_rows
        scores = block_scores(query_rot, key_rot, start, seq_length, score_scale)
        probs = jnp.exp(scores - lse_blocks[index][:, :, None])
        dprobs = jnp.einsum(
            "qhw,khw->hqk", dattended_low, mixed, preferred_element_type=jnp.float32
        )
        inner = jnp.sum(probs * dprobs, axis=2, keepdims=True)
        dscore_low = (probs * (dprobs - inner)).astype(jnp.bfloat16)
        dquery_blk = (
            jnp.einsum("hqk,khw->qhw", dscore_low, key_rot, preferred_element_type=jnp.float32)
            * score_scale
        )
        dkey_total = (
            dkey_total
            + jnp.einsum("hqk,qhw->khw", dscore_low, query_rot, preferred_element_type=jnp.float32)
            * score_scale
        )
        dmixed_total = dmixed_total + jnp.einsum(
            "hqk,qhw->khw",
            probs.astype(jnp.bfloat16),
            dattended_low,
            preferred_element_type=jnp.float32,
        )
        return ((dkey_total, dmixed_total), dquery_blk)

    zero_heads = jnp.zeros((seq_rows, HEADS, HEAD), jnp.float32)
    (dkey_rot, dmixed), dquery_blocks = lax.scan(
        backward_block, (zero_heads, zero_heads), jnp.arange(block_count, dtype=jnp.int32)
    )
    dquery_rot = dquery_blocks.reshape(seq_rows, HEADS, HEAD)
    dquery_low = (
        unrotate(dquery_rot, cosine, sine).astype(jnp.bfloat16).reshape(seq_rows, HEADS * HEAD)
    )
    dkey_low = unrotate(dkey_rot, cosine, sine).astype(jnp.bfloat16).reshape(seq_rows, HEADS * HEAD)
    dvalues_low = (
        (value_gate[..., None] * dmixed[:, :, None, :])
        .astype(jnp.bfloat16)
        .reshape(seq_rows, HEADS * AEXP * HEAD)
    )
    dvalue_gate = jnp.sum(dmixed[:, :, None, :] * values_all, axis=3)
    dvalue_logit = (
        (dvalue_gate * value_mask * value_sig * (1.0 - value_sig))
        .astype(jnp.bfloat16)
        .reshape(seq_rows, HEADS * AEXP)
    )
    grad_query = contract_rows(normed_low, dquery_low)
    grad_key = contract_rows(normed_low, dkey_low)
    grad_value = contract_rows(tokens, dvalues_low)
    grad_value_router = contract_rows(tokens, dvalue_logit)
    grad_output_router = contract_rows(tokens, doutput_logit)
    dnormed = contract_cols(dquery_low, query_weight) + contract_cols(dkey_low, key_weight)
    grad_gain = jnp.sum(dnormed * scaled, axis=0)
    dscaled = dnormed * norm_gain
    dnorm_in = inverse_std * (
        dscaled
        - jnp.mean(dscaled, axis=1, keepdims=True)
        - scaled * jnp.mean(dscaled * scaled, axis=1, keepdims=True)
    )
    dinput_rest = (
        contract_cols(dvalues_low, value_weight)
        + contract_cols(dvalue_logit, value_router)
        + contract_cols(doutput_logit, output_router)
    )
    grad_tokens = (dhidden + dnorm_in + dinput_rest).astype(jnp.bfloat16)
    shares = tuple(
        (
            lax.psum_scatter(grad_gain, ("dp", "expert"), scatter_dimension=0, tiled=True),
            lax.psum_scatter(grad_query, ("dp", "expert"), scatter_dimension=0, tiled=True),
            lax.psum_scatter(grad_key, ("dp", "expert"), scatter_dimension=0, tiled=True),
            lax.psum_scatter(grad_value, ("dp", "expert"), scatter_dimension=0, tiled=True),
            lax.psum_scatter(grad_output, ("dp", "expert"), scatter_dimension=0, tiled=True),
            lax.psum_scatter(grad_value_router, ("dp", "expert"), scatter_dimension=0, tiled=True),
            lax.psum_scatter(grad_output_router, ("dp", "expert"), scatter_dimension=0, tiled=True),
            lax.psum_scatter(grad_router, ("dp", "expert"), scatter_dimension=0, tiled=True),
        )
    )
    expert_shares = tuple(
        (
            lax.psum_scatter(
                grad_up.astype(jnp.bfloat16), "dp", scatter_dimension=1, tiled=True
            ).astype(jnp.float32),
            lax.psum_scatter(
                grad_down.astype(jnp.bfloat16), "dp", scatter_dimension=1, tiled=True
            ).astype(jnp.float32),
        )
    )
    local_counts = jnp.sum(member * valid_int[:, None], axis=0, dtype=jnp.int32)
    summed_counts = lax.psum_scatter(
        local_counts, ("dp", "expert"), scatter_dimension=0, tiled=True
    )
    counts = running_counts + summed_counts
    return (output, grad_tokens) + shares + expert_shares + (counts,)


def solution(mesh):
    in_specs = (
        P(("dp", "expert"), None),
        P(),
        P(),
        P(),
        P(),
        P(),
        P(),
        P(),
        P(),
        P("expert", None, None),
        P("expert", None, None),
        P(("dp", "expert")),
        P(("dp", "expert"), None, None),
        P(("dp", "expert"), None, None),
        P(("dp", "expert"), None),
        P(("dp", "expert")),
        P(("dp", "expert"), None),
    )
    out_specs = (
        P(("dp", "expert"), None),
        P(("dp", "expert"), None),
        P(("dp", "expert")),
        P(("dp", "expert"), None),
        P(("dp", "expert"), None),
        P(("dp", "expert"), None),
        P(("dp", "expert"), None),
        P(("dp", "expert"), None),
        P(("dp", "expert"), None),
        P(("dp", "expert"), None),
        P("expert", "dp", None),
        P("expert", "dp", None),
        P(("dp", "expert")),
    )
    return jax.shard_map(shards, mesh=mesh, in_specs=in_specs, out_specs=out_specs, check_vma=False)
```

profile of v0, /device:TPU:0, one launch (start us, length us, event | category | flops | bytes accessed | tf_op | source)
XLA Modules:
  0.0 2559.2 jit_solution(13225649356724532386)
XLA Ops:
  19.8 32.8 %gather_fusion.5 = s32[4096]{0:T(1024)S(1)} fusion(s32[256,192]{1,0:T(8,128)S(1)} %bitcast_subtract_fusion, s32[4096]{0:T(1024)S(1)} %reshape.350), kind=kCustom, calls=%fused_computation.5 | custom fusion | bytes 65536 | tf_op jit(solution)/shard_map/jit(take_along_axis)/gather | solution.py:50
  53.0 15.8 scatter_custom_fusion
  84.3 26.8 %gather_fusion = bf16[6144,1024]{1,0:T(8,128)(2,1)} fusion(bf16[257,1024]{1,0:T(8,128)(2,1)S(1)} %concatenate.24, s32[6144]{0:T(1024)S(1)} %get-tuple-element.168), kind=kCustom, calls=%fused_computation | custom fusion | bytes 25190400 | tf_op jit(solution)/shard_map/gather | solution.py:197
  111.1 281.5 %all_to_all.20 = bf16[8,24,32,1024]{3,2,1,0:T(8,128)(2,1)} all-to-all(bf16[8,24,32,1024]{3,2,1,0:T(8,128)(2,1)} %bitcast.174), channel_id=1, replica_groups=mesh['dp'=4,'expert'=8] {'expert'}, dimensions={0} | all-to-all | bytes 25165824 | tf_op jit(solution)/shard_map/all_to_all | solution.py:204
  392.6 12.0 fusion.19
  404.6 11.2 convert_bitcast_fusion.1
  415.8 10.9 copy.242
  434.4 33.0 %gather_fusion.4 = f32[4096]{0:T(1024)S(1)} fusion(f32[256,192]{0,1:T(8,128)S(1)} %fusion.39, s32[4096]{0:T(1024)S(1)} %reshape.350), kind=kCustom, calls=%fused_computation.4 | custom fusion | bytes 65536 | tf_op jit(solution)/shard_map/jit(take_along_axis)/gather | solution.py:194
  467.6 237.8 %all-to-all-done.1 = bf16[8,24,32,1024]{3,2,1,0:T(8,128)(2,1)} async-done(((bf16[8,24,32,1024]{3,2,1,0:T(8,128)(2,1)}), bf16[8,24,32,1024]{3,2,1,0:T(8,128)(2,1)}, u32[]{:S(2)}, u32[]{:S(2)}) %all-to-all-start.1) | async-done | bytes 12582944 | tf_op jit(solution)/shard_map/all_to_all | solution.py:206
  705.4 27.0 %gather_fusion.1 = bf16[4096,1024]{1,0:T(8,128)(2,1)} fusion(bf16[6144,1024]{1,0:T(8,128)(2,1)} %bitcast.18, s32[4096]{0:T(1024)S(1)} %broadcast_clamp_fusion), kind=kCustom, calls=%fused_computation.1 | custom fusion | bytes 16793600 | tf_op jit(solution)/shard_map/gather | solution.py:212
  750.5 35.1 %gather_fusion.2 = bf16[6144,1024]{1,0:T(8,128)(2,1)} fusion(bf16[4097,1024]{1,0:T(8,128)(2,1)} %concatenate.25, s32[6144]{0:T(1024)S(1)} %copy-done.54), kind=kCustom, calls=%fused_computation.2 | custom fusion | bytes 25190400 | tf_op jit(solution)/shard_map/gather | solution.py:203
  785.6 277.7 %all_to_all.21 = bf16[8,24,32,1024]{3,2,1,0:T(8,128)(2,1)S(1)} all-to-all(bf16[8,24,32,1024]{3,2,1,0:T(8,128)(2,1)} %bitcast.175), channel_id=1, replica_groups=mesh['dp'=4,'expert'=8] {'expert'}, dimensions={0} | all-to-all | bytes 25165824 | tf_op jit(solution)/shard_map/all_to_all | solution.py:207
  1085.0 10.9 copy.246
  1121.4 252.1 %all-to-all-done.3 = bf16[8,24,32,1024]{3,2,1,0:T(8,128)(2,1)} async-done(((bf16[8,24,32,1024]{3,2,1,0:T(8,128)(2,1)}), bf16[8,24,32,1024]{3,2,1,0:T(8,128)(2,1)}, u32[]{:S(2)}, u32[]{:S(2)}) %all-to-all-start.3) | async-done | bytes 12582944 | tf_op jit(solution)/shard_map/all_to_all | solution.py:211
  1373.5 27.0 %gather_fusion.3 = bf16[4096,1024]{1,0:T(8,128)(2,1)} fusion(bf16[6144,1024]{1,0:T(8,128)(2,1)} %bitcast.27, s32[4096]{0:T(1024)S(1)} %broadcast_clamp_fusion), kind=kCustom, calls=%fused_computation.3 | custom fusion | bytes 16793600 | tf_op jit(solution)/shard_map/gather | solution.py:221
  1450.6 11.6 copy.285
  1463.2 37.8 %all-reduce.3 = s32[192]{0:T(256)S(1)} all-reduce(s32[192]{0:T(256)S(1)} %multiply_reduce_fusion.6), channel_id=12, replica_groups=mesh['dp'=4,'expert'=8] {'dp','expert'}, use_global_device_ids=true, to_apply=%region_31.32.clone | all-reduce | flops 192 | bytes 1536
  1516.9 41.8 %all-reduce.2 = f32[1024]{0:T(1024)S(1)} all-reduce(f32[1024]{0:T(1024)S(1)} %get-tuple-element.144), channel_id=2, replica_groups=mesh['dp'=4,'expert'=8] {'dp','expert'}, use_global_device_ids=true, to_apply=%region_20.21.clone | all-reduce | flops 1024 | bytes 8192
  1566.9 119.5 %reduce-scatter.30.cloned.1.call-done = f32[32,20]{1,0:T(8,128)} async-done(((f32[1024,20]{1,0:T(8,128)}), f32[32,20]{1,0:T(8,128)}) %reduce-scatter.30.cloned.1.call-update) | async-done | bytes 2576
  1687.8 132.8 %reduce-scatter.22.cloned.1.call-done = f32[32,192]{1,0:T(8,128)} async-done(((f32[1024,192]{1,0:T(8,128)}), f32[32,192]{1,0:T(8,128)}) %reduce-scatter.22.cloned.1.call-update) | async-done | bytes 24592 | tf_op jit(solution)/shard_map/reduce_scatter | solution.py:312
  1820.6 137.2 %reduce-scatter.18.cloned.1.call-done = f32[32,512]{1,0:T(8,128)} async-done(((f32[1024,512]{1,0:T(8,128)}), f32[32,512]{1,0:T(8,128)}) %reduce-scatter.18.cloned.1.call-update) | async-done | bytes 65552 | tf_op jit(solution)/shard_map/reduce_scatter | solution.py:307
  1957.8 137.1 %reduce-scatter.16.cloned.1.call-done = f32[32,512]{1,0:T(8,128)} async-done(((f32[1024,512]{1,0:T(8,128)}), f32[32,512]{1,0:T(8,128)}) %reduce-scatter.16.cloned.1.call-update) | async-done | bytes 65552 | tf_op jit(solution)/shard_map/reduce_scatter | solution.py:306
  2094.9 227.4 %reduce-scatter.20.cloned.1.call-done = f32[32,2560]{1,0:T(8,128)} async-done(((f32[1024,2560]{1,0:T(8,128)}), f32[32,2560]{1,0:T(8,128)}) %reduce-scatter.20.cloned.1.call-update) | async-done | bytes 327696 | tf_op jit(solution)/shard_map/reduce_scatter | solution.py:309
  2322.4 229.8 %reduce-scatter.28.cloned.1.call-done = f32[32,2560]{1,0:T(8,128)} async-done(((f32[1024,2560]{1,0:T(8,128)}), f32[32,2560]{1,0:T(8,128)}) %reduce-scatter.28.cloned.1.call-update) | async-done | bytes 327696
  (292 shorter events, 176.3 us)
Async XLA Ops:
  7.2 62.2 %copy-start = (bf16[1024,512]{1,0:T(8,128)(2,1)S(1)}, bf16[1024,512]{1,0:T(8,128)(2,1)}, u32[]{:S(2)}) copy-start(bf16[1024,512]{1,0:T(8,128)(2,1)} %param.20) | copy-start | bytes 3145732
  11.0 59.2 %copy-start.57 = (f32[256]{0:T(256)}, f32[256]{0:T(256)S(1)}, u32[]{:S(2)}) copy-start(f32[256]{0:T(256)S(1)} %broadcast_multiply_fusion.2) | copy-start | bytes 3076
  12.3 57.1 %copy-start.61 = (f32[256]{0:T(256)}, f32[256]{0:T(256)S(1)}, u32[]{:S(2)}) copy-start(f32[256]{0:T(256)S(1)} %add_rsqrt_fusion) | copy-start | bytes 3076
  17.0 62.7 %copy-start.40 = (f32[256,4,5]{0,2,1:T(8,128)}, f32[256,4,5]{0,2,1:T(8,128)S(1)}, u32[]{:S(2)}) copy-start(f32[256,4,5]{0,2,1:T(8,128)S(1)} %copy.223) | copy-start | bytes 61444
  17.1 62.0 %copy-start.38 = (f32[256,4,5]{0,2,1:T(8,128)}, f32[256,4,5]{0,2,1:T(8,128)S(1)}, u32[]{:S(2)}) copy-start(f32[256,4,5]{0,2,1:T(8,128)S(1)} %copy.226) | copy-start | bytes 61444
  19.7 57.7 %copy-start.29 = (f32[256,64]{1,0:T(8,128)}, f32[256,64]{1,0:T(8,128)S(1)}, u32[]{:S(2)}) copy-start(f32[256,64]{1,0:T(8,128)S(1)} %get-tuple-element.171) | copy-start | bytes 196612
  19.7 57.7 %copy-start.31 = (f32[256,64]{1,0:T(8,128)}, f32[256,64]{1,0:T(8,128)S(1)}, u32[]{:S(2)}) copy-start(f32[256,64]{1,0:T(8,128)S(1)} %get-tuple-element.172) | copy-start | bytes 196612
  19.8 49.6 %copy-start.1 = (bf16[256,1024]{1,0:T(8,128)(2,1)S(1)}, bf16[256,1024]{1,0:T(8,128)(2,1)}, u32[]{:S(2)}) copy-start(bf16[256,1024]{1,0:T(8,128)(2,1)} %param.17) | copy-start | bytes 1572868
  19.8 49.6 %copy-start.55 = (f32[1024]{0:T(1024)S(1)}, f32[1024]{0:T(1024)}, u32[]{:S(2)}) copy-start(f32[1024]{0:T(1024)} %param.18) | copy-start | bytes 12292
  84.2 348.8 %copy-start.21 = (bf16[256,1024]{1,0:T(8,128)(2,1)}, bf16[256,1024]{1,0:T(8,128)(2,1)S(1)}, u32[]{:S(2)}) copy-start(bf16[256,1024]{1,0:T(8,128)(2,1)S(1)} %get-tuple-element.175) | copy-start | bytes 1572868
  426.7 278.6 %all-to-all-start.1 = ((bf16[8,24,32,1024]{3,2,1,0:T(8,128)(2,1)}), bf16[8,24,32,1024]{3,2,1,0:T(8,128)(2,1)}, u32[]{:S(2)}, u32[]{:S(2)}) async-start(bf16[8,24,32,1024]{3,2,1,0:T(8,128)(2,1)} %copy.242), calls=%async_computation.1 | async-start | bytes 25165824 | tf_op jit(solution)/shard_map/all_to_all | solution.py:206
  785.6 282.2 %copy-start.67 = (f32[24,8,32,128]{3,2,1,0:T(8,128)S(1)}, f32[24,8,32,128]{3,2,1,0:T(8,128)}, u32[]{:S(2)}) copy-start(f32[24,8,32,128]{3,2,1,0:T(8,128)} %get-tuple-element.178) | copy-start | bytes 9437188
  1095.9 277.6 %all-to-all-start.3 = ((bf16[8,24,32,1024]{3,2,1,0:T(8,128)(2,1)}), bf16[8,24,32,1024]{3,2,1,0:T(8,128)(2,1)}, u32[]{:S(2)}, u32[]{:S(2)}) async-start(bf16[8,24,32,1024]{3,2,1,0:T(8,128)(2,1)} %copy.246), calls=%async_computation.3 | async-start | bytes 25165824 | tf_op jit(solution)/shard_map/all_to_all | solution.py:211
  1101.4 406.3 %reduce-scatter.26.cloned.1.call-start = ((), (), s32[]{:S(2)}) async-start(), calls=%async_computation.18 | async-start | bytes 7864320 | tf_op jit(solution)/shard_map/reduce_scatter | solution.py:320
  1110.0 401.1 %reduce-scatter.24.cloned.1.call-start = ((), (), s32[]{:S(2)}) async-start(), calls=%async_computation.17 | async-start | bytes 7864320 | tf_op jit(solution)/shard_map/reduce_scatter | solution.py:317
  1120.3 445.3 %reduce-scatter.32.cloned.1.call-start = ((), (), s32[]{:S(2)}) async-start(), calls=%async_computation.21 | async-start | bytes 540672
  1421.2 265.2 %reduce-scatter.30.cloned.1.call-start = ((), (), s32[]{:S(2)}) async-start(), calls=%async_computation.20 | async-start | bytes 540672
  1424.1 396.6 %reduce-scatter.22.cloned.1.call-start = ((), (), s32[]{:S(2)}) async-start(), calls=%async_computation.16 | async-start | bytes 1081344 | tf_op jit(solution)/shard_map/reduce_scatter | solution.py:312
  1425.5 532.3 %reduce-scatter.18.cloned.1.call-start = ((), (), s32[]{:S(2)}) async-start(), calls=%async_computation.14 | async-start | bytes 2162688 | tf_op jit(solution)/shard_map/reduce_scatter | solution.py:307
  1431.8 663.1 %reduce-scatter.16.cloned.1.call-start = ((), (), s32[]{:S(2)}) async-start(), calls=%async_computation.13 | async-start | bytes 2162688 | tf_op jit(solution)/shard_map/reduce_scatter | solution.py:306
  1436.8 885.6 %reduce-scatter.20.cloned.1.call-start = ((), (), s32[]{:S(2)}) async-start(), calls=%async_computation.15 | async-start | bytes 10813440 | tf_op jit(solution)/shard_map/reduce_scatter | solution.py:309
  1443.8 1108.4 %reduce-scatter.28.cloned.1.call-start = ((), (), s32[]{:S(2)}) async-start(), calls=%async_computation.19 | async-start | bytes 10813440
  1462.2 38.9 %copy-start.66 = (s32[6]{0:T(128)S(1)}, s32[6]{0:T(128)}, u32[]{:S(2)}) copy-start(s32[6]{0:T(128)} %param.32) | copy-start | bytes 76
  1462.2 39.5 %copy-start.53 = (f32[256,16]{0,1:T(8,128)S(1)}, f32[256,16]{0,1:T(8,128)}, u32[]{:S(2)}) copy-start(f32[256,16]{0,1:T(8,128)} %copy-done.52) | copy-start | bytes 49156
  (57 other events, 211.5 us)
Sparse Core Ops, SparseCore 0:
  1110.2 59.0 reduce-scatter.25
  1172.0 58.3 reduce-scatter.23
  1421.3 132.6 reduce-scatter.31
  1556.2 130.1 reduce-scatter.29
  1689.1 131.4 reduce-scatter.21
  1823.4 134.3 reduce-scatter.17
  1960.6 134.2 reduce-scatter.15
  2097.9 224.4 reduce-scatter.19
  2325.3 226.7 reduce-scatter.27
where the time goes:
time: 2560 us
  waiting for transfers between devices  1470 us (57%)
  blocking collectives  639 us (25%)
  local copies, waits for them, and re-layouts  261 us (10%)
  matrix products  119 us (5%)
  other arithmetic  36.9 us (1%)
    unnamed x12, waiting for transfers between devices  349 us
    all_to_all x1, blocking collectives, shards(): lax.all_to_all(send_rows, 'expert', split_axis=0, concat_axis=0, tiled=True)  282 us
    all_to_all x1, blocking collectives, shards(): lax.all_to_all(grad_send, 'expert', split_axis=0, concat_axis=0, tiled=True)  278 us
    all_to_all x1, waiting for transfers between devices, shards(): lax.all_to_all(drows_expert, 'expert', split_axis=0, concat_axis=0, tiled...  252 us
    all_to_all x1, waiting for transfers between devices, shards(): lax.all_to_all(expert_rows, 'expert', split_axis=0, concat_axis=0, tiled=...  238 us
    reduce_scatter x1, waiting for transfers between devices, shards(): lax.psum_scatter(grad_output, ('dp', 'expert'), scatter_dimension=0, tile...  227 us
    reduce_scatter x1, waiting for transfers between devices, shards(): lax.psum_scatter(grad_key, ('dp', 'expert'), scatter_dimension=0, tiled=T...  137 us
    reduce_scatter x1, waiting for transfers between devices, shards(): lax.psum_scatter(grad_query, ('dp', 'expert'), scatter_dimension=0, tiled...  137 us
  transfers between devices with their start and end apart: 11, of which 8 were waited for; matrix products, arithmetic and copies ran while one was open for 6% of the time, Pallas kernels for 0%

commit v1 on v0

v1 whole, which is shorter than its diff:
```python
import functools
import math

import jax
import jax.numpy as jnp
from jax import lax
from jax.experimental import pallas as pl
from jax.experimental.pallas import tpu as pltpu
from jax.sharding import PartitionSpec as P

HEADS = 4
HEAD = 128
AEXP = 5
BF = jnp.bfloat16
F32 = jnp.float32
VMEM_LIMIT = 60 * 1024 * 1024
GELU_C = math.sqrt(2.0 / math.pi)
GELU_K = 0.044715


def rope_tables(seq_rows, head_width):
    half_width = head_width // 2
    ladder = jnp.arange(half_width, dtype=jnp.float32) * (2.0 / head_width)
    freqs = jnp.exp(-math.log(10000.0) * ladder)
    angles = jnp.arange(seq_rows, dtype=jnp.float32)[:, None] * freqs[None, :]
    return (jnp.cos(angles), jnp.sin(angles))


def rotate(vectors, cosine, sine):
    half_width = vectors.shape[-1] // 2
    former = vectors[..., :half_width]
    latter = vectors[..., half_width:]
    cos_rows = cosine[:, None, :]
    sin_rows = sine[:, None, :]
    return jnp.concatenate(
        [former * cos_rows - latter * sin_rows, former * sin_rows + latter * cos_rows], axis=-1
    )


def unrotate(grads, cosine, sine):
    half_width = grads.shape[-1] // 2
    former = grads[..., :half_width]
    latter = grads[..., half_width:]
    cos_rows = cosine[:, None, :]
    sin_rows = sine[:, None, :]
    return jnp.concatenate(
        [former * cos_rows + latter * sin_rows, latter * cos_rows - former * sin_rows], axis=-1
    )


def contract_rows(left, right):
    return lax.dot_general(
        left, right, (((0,), (0,)), ((), ())), preferred_element_type=jnp.float32
    )


def contract_cols(left, right):
    return lax.dot_general(
        left, right, (((1,), (1,)), ((), ())), preferred_element_type=jnp.float32
    )


class Grid:
    def __init__(self, size):
        self.hi = 4
        self.lo = size // 4
        self.size = size

    def hi_shift(self, x):
        pairs = [
            (i, ((i // self.lo + 1) % self.hi) * self.lo + i % self.lo) for i in range(self.size)
        ]
        return lax.ppermute(x, "expert", pairs)

    def lo_shift(self, x):
        pairs = [
            (i, (i // self.lo) * self.lo + (i % self.lo + 1) % self.lo) for i in range(self.size)
        ]
        return lax.ppermute(x, "expert", pairs)

    def sources(self):
        me = lax.axis_index("expert")
        h, l = me // self.lo, me % self.lo
        return [
            ((h + self.hi - dh) % self.hi) * self.lo + (l + self.lo - dl) % self.lo
            for dh in range(self.hi)
            for dl in range(self.lo)
        ]

    def all_rows(self, block):
        rows = {(0, 0): block}
        for step in range(self.hi + self.lo - 2):
            fresh = {}
            for dh in range(self.hi):
                for dl in range(self.lo):
                    if dh + dl == step + 1:
                        if dl > 0:
                            fresh[(dh, dl)] = self.lo_shift(rows[(dh, dl - 1)])
                        else:
                            fresh[(dh, dl)] = self.hi_shift(rows[(dh - 1, dl)])
            keys = list(fresh)
            rows.update(zip(keys, lax.optimization_barrier(tuple(fresh[k] for k in keys))))
        return [rows[(dh, dl)] for dh in range(self.hi) for dl in range(self.lo)]

    def sum_rows(self, parts):
        def part(a, b):
            return parts[((self.hi - a) % self.hi) * self.lo + (self.lo - b) % self.lo]

        sums = []
        for a in range(self.hi - 1, -1, -1):
            acc = part(a, self.lo - 1)
            for b in range(self.lo - 2, -1, -1):
                acc = add(part(a, b), self.lo_shift(acc))
            sums.append(acc)
        acc = sums[0]
        for s in range(1, self.hi):
            acc = add(sums[s], self.hi_shift(acc))
        return acc


def add(a, b):
    return (a.astype(F32) + b.astype(F32)).astype(BF)


class Tree:
    def __init__(self, dp, grid):
        self.grid = grid
        self.dp = dp
        self.xs = dp // 2

    def coords(self):
        dp, ex = lax.axis_index("dp"), lax.axis_index("expert")
        return jnp.stack([dp % 2, dp // 2, ex % self.grid.lo, ex // self.grid.lo])

    def core_shift(self, x):
        return lax.ppermute(x, "dp", [(i, i ^ 1) for i in range(self.dp)])

    def x_shift(self, x):
        pairs = [(i, (i // 2 + 1) % self.xs * 2 + i % 2) for i in range(self.dp)]
        return lax.ppermute(x, "dp", pairs)

    def ring(self, parts, shift):
        acc = parts[-1]
        for b in range(len(parts) - 2, -1, -1):
            acc = add(parts[b], shift(acc))
        return acc

    def sum_rows(self, near, far):
        got = self.core_shift(far)
        lo, hi = self.grid.lo, self.grid.hi
        acc = self.ring([add(near[i], got[i]) for i in range(self.xs)], self.x_shift)
        acc = self.ring([acc[i] for i in range(lo)], self.grid.lo_shift)
        acc, last = self.ring_but_last([acc[i] for i in range(hi)], self.grid.hi_shift)
        return acc.astype(F32) + last.astype(F32)

    def ring_but_last(self, parts, shift):
        acc = parts[-1]
        for b in range(len(parts) - 2, 0, -1):
            acc = add(parts[b], shift(acc))
        return shift(acc), parts[0]


def gather_kernel(count, cap, *refs):
    rows, slots, out = refs[:count], refs[count : 2 * count], refs[2 * count]
    experts = out.shape[0]
    seq_rows = slots[0].shape[1]
    step = 8
    for i in range(count):
        for e0 in range(0, experts, step):
            idx = slots[i][e0 : e0 + step, :]
            place = lax.broadcasted_iota(jnp.int32, (step, cap, seq_rows), 1).astype(F32)
            pick = (idx[:, None, :] == place).astype(F32).astype(BF).reshape(step * cap, seq_rows)
            got = jnp.dot(pick, rows[i][:seq_rows, :], preferred_element_type=F32)
            out[e0 : e0 + step, i * cap : (i + 1) * cap, :] = got.astype(BF).reshape(
                step, cap, got.shape[1]
            )


def gather_call(rows, slots, cap):
    count = len(rows)
    experts = slots[0].shape[0]
    width = rows[0].shape[1]
    flops = 2 * count * experts * cap * slots[0].shape[1] * width
    return pl.pallas_call(
        functools.partial(gather_kernel, count, cap),
        out_shape=jax.ShapeDtypeStruct((experts, count * cap, width), BF),
        compiler_params=pltpu.CompilerParams(vmem_limit_bytes=40 * 1024 * 1024),
        cost_estimate=pl.CostEstimate(
            flops=flops, bytes_accessed=2 * experts * count * cap * width, transcendentals=0
        ),
        name="gather_rows",
    )(*rows, *slots)


def expert_kernel(groups, per, cap, at_ref, *refs):
    n = groups // per
    xs_in, gs_in = refs[:n], refs[n : 2 * n]
    up, down, router, slot = refs[2 * n : 2 * n + 4]
    outs = refs[2 * n + 4 :]
    moe = outs[:groups]
    dhid = outs[groups : 2 * groups]
    near, far, grt = outs[2 * groups : 2 * groups + 3]
    xs, gs, w, d2, rw, dr, gacc = outs[2 * groups + 3 :]
    e = pl.program_id(0)
    ff = up.shape[2]

    @pl.when(e == 0)
    def _():
        w[:, ff:] = router[...]
        grt[...] = jnp.zeros_like(grt)

    for i in range(n):
        xs[i * per * cap : (i + 1) * per * cap, :] = xs_in[i][0]
        gs[i * per * cap : (i + 1) * per * cap, :] = gs_in[i][0]
    w[:, :ff] = up[0]
    both = jnp.dot(xs[...], w[...], preferred_element_type=F32)
    pre = both[:, :ff]
    sel = lax.broadcasted_iota(jnp.int32, pre.shape, 1) == e
    chosen = jnp.sum(jnp.where(sel, jax.nn.sigmoid(both[:, ff:]), 0.0), axis=1, keepdims=True)
    square = pre * pre
    t = jnp.tanh(GELU_C * (pre + GELU_K * (square * pre)))
    half = 0.5 * (1.0 + t)
    act = (half * pre).astype(BF)
    slope = half + 0.5 * pre * (1.0 - t * t) * (GELU_C * (1.0 + 3.0 * GELU_K * square))
    u = jnp.dot(gs[...], down[0], preferred_element_type=F32)
    act32 = act.astype(F32)
    dchosen = jnp.sum(u * act32, axis=1, keepdims=True)
    drl = dchosen * chosen * (1.0 - chosen)
    a2 = (chosen * act32).astype(BF)
    d2[:, :ff] = (chosen * u * slope).astype(BF)
    d2[:, ff:] = jnp.where(sel, drl, 0.0).astype(BF)
    got = lax.dot_general(
        a2, down[0], (((1,), (1,)), ((), ())), preferred_element_type=F32
    ).astype(BF)
    dgot = lax.dot_general(
        d2[...], w[...], (((1,), (1,)), ((), ())), preferred_element_type=F32
    ).astype(BF)
    at = pl.multiple_of(e * cap, cap)
    for s in range(groups):
        rw[s, pl.ds(at, cap), :] = got[s * cap : (s + 1) * cap]
        dr[s, pl.ds(at, cap), :] = dgot[s * cap : (s + 1) * cap]
    gu = lax.dot_general(d2[...], xs[...], (((0,), (0,)), ((), ())), preferred_element_type=F32)
    gacc[0] = gu[:ff]
    grt[...] += gu[ff : ff + grt.shape[0]]
    gacc[1] = lax.dot_general(a2, gs[...], (((0,), (0,)), ((), ())), preferred_element_type=F32)
    x_size, _, _, _, lanes = near.shape
    for xr in range(x_size):
        base = lax.rem(at_ref[1] + xr, x_size) * 2
        for cr, out in enumerate((near, far)):
            cut = pl.multiple_of((base + lax.rem(at_ref[0] + cr, 2)) * lanes, lanes)
            for i in range(2):
                out[xr, 0, i] = gacc[i, :, pl.ds(cut, lanes)].astype(BF)

    @pl.when(e == pl.num_programs(0) - 1)
    def _():
        experts = slot.shape[2]
        total = experts * cap
        rowi = lax.broadcasted_iota(jnp.int32, (experts, total), 0)
        coli = lax.broadcasted_iota(jnp.int32, (experts, total), 1)
        spread = (coli // cap == rowi).astype(F32).astype(BF)
        for s in range(groups):
            wide = jnp.dot(slot[s], spread, preferred_element_type=F32)
            lane = lax.broadcasted_iota(jnp.int32, wide.shape, 1) % cap
            put = (wide == lane.astype(F32)).astype(F32).astype(BF)
            dhid[s][...] = jnp.dot(put, dr[s], preferred_element_type=F32).astype(BF)
            moe[s][...] = jnp.dot(put, rw[s], preferred_element_type=F32).astype(BF)


def expert_call(coords, x_size, xs, gs, up, down, router, slot, cap):
    n = len(xs)
    experts, width, ff = up.shape
    groups, seq_rows, _ = slot.shape
    per = groups // n
    rows = groups * cap
    pad = -(-experts // 8) * 8
    lanes = width // (2 * x_size)
    row_spec = pl.BlockSpec((1, per * cap, width), lambda e, _: (e, 0, 0))
    w_spec = pl.BlockSpec((1, width, ff), lambda e, _: (e, 0, 0))
    whole = lambda *shape: pl.BlockSpec(shape, lambda e, _: (0,) * len(shape))
    g_spec = pl.BlockSpec((x_size, 1, 2, ff, lanes), lambda e, _: (0, e, 0, 0, 0))
    one = jax.ShapeDtypeStruct((seq_rows, width), BF)
    flops = experts * rows * width * ff * 2 * 8 + 4 * groups * seq_rows * experts * cap * width
    outs = pl.pallas_call(
        functools.partial(expert_kernel, groups, per, cap),
        grid_spec=pltpu.PrefetchScalarGridSpec(
            num_scalar_prefetch=1,
            grid=(experts,),
            in_specs=[row_spec] * (2 * n)
            + [w_spec, w_spec, whole(width, ff), whole(groups, seq_rows, experts)],
            out_specs=[whole(seq_rows, width)] * (2 * groups) + [g_spec, g_spec, whole(pad, width)],
            scratch_shapes=[
                pltpu.VMEM((rows, width), BF),
                pltpu.VMEM((rows, width), BF),
                pltpu.VMEM((width, 2 * ff), BF),
                pltpu.VMEM((rows, 2 * ff), BF),
                pltpu.VMEM((groups, experts * cap, width), BF),
                pltpu.VMEM((groups, experts * cap, width), BF),
                pltpu.VMEM((2, ff, width), F32),
            ],
        ),
        out_shape=[one] * (2 * groups)
        + [jax.ShapeDtypeStruct((x_size, experts, 2, ff, lanes), BF)] * 2
        + [jax.ShapeDtypeStruct((pad, width), F32)],
        compiler_params=pltpu.CompilerParams(vmem_limit_bytes=VMEM_LIMIT),
        cost_estimate=pl.CostEstimate(
            flops=flops, bytes_accessed=experts * rows * width * 8, transcendentals=0
        ),
        name="experts",
    )(coords, *xs, *gs, up, down, router, slot)
    return outs[:groups], outs[groups : 2 * groups], outs[-3], outs[-2], outs[-1]


def spread_kernel(sizes, rows, at_ref, *refs):
    left, right = refs[0], refs[1]
    extra = refs[2] if len(refs) == 7 else None
    near, far, turned, res = refs[-4:]
    x_size, lo, hi = sizes

    @pl.when(pl.program_id(0) == 0)
    def _():
        turned[...] = jnp.transpose(left[...])

    got = jnp.dot(turned[...], right[...], preferred_element_type=F32)
    res[...] = got if extra is None else got + extra[...].astype(F32)
    for cr, out in enumerate((near, far)):
        core = lax.rem(at_ref[0] + cr, 2)
        for xr in range(x_size):
            x = lax.rem(at_ref[1] + xr, x_size)
            for lr in range(lo):
                l = lax.rem(at_ref[2] + lr, lo)
                for hr in range(hi):
                    h = lax.rem(at_ref[3] + hr, hi)
                    start = (((x * 2 + core) * hi + h) * lo + l) * rows
                    out[xr, lr, hr] = res[pl.ds(pl.multiple_of(start, rows), rows), :].astype(BF)


def spread_call(coords, tree, left, right, tile, extra=None):
    seq_rows, width = left.shape
    cols = right.shape[1]
    sizes = (tree.xs, tree.grid.lo, tree.grid.hi)
    rows = width // (tree.dp * tree.grid.size)
    o_spec = pl.BlockSpec((*sizes, rows, tile), lambda j, _: (0, 0, 0, 0, j))
    in_specs = [
        pl.BlockSpec((seq_rows, width), lambda j, _: (0, 0)),
        pl.BlockSpec((seq_rows, tile), lambda j, _: (0, j)),
    ]
    args = [left, right]
    if extra is not None:
        in_specs.append(pl.BlockSpec((width, tile), lambda j, _: (0, j)))
        args.append(extra)
    return pl.pallas_call(
        functools.partial(spread_kernel, sizes, rows),
        grid_spec=pltpu.PrefetchScalarGridSpec(
            num_scalar_prefetch=1,
            grid=(cols // tile,),
            in_specs=in_specs,
            out_specs=[o_spec, o_spec],
            scratch_shapes=[pltpu.VMEM((width, seq_rows), BF), pltpu.VMEM((width, tile), F32)],
        ),
        out_shape=[jax.ShapeDtypeStruct((*sizes, rows, cols), BF)] * 2,
        compiler_params=pltpu.CompilerParams(vmem_limit_bytes=40 * 1024 * 1024),
        cost_estimate=pl.CostEstimate(
            flops=2 * seq_rows * width * cols, bytes_accessed=2 * width * cols, transcendentals=0
        ),
        name="weight_grad",
    )(coords, *args)


def shards(
    tokens,
    norm_gain,
    query_weight,
    key_weight,
    value_weight,
    output_weight,
    value_router,
    output_router,
    expert_router,
    expert_up,
    expert_down,
    lengths,
    value_choice,
    output_choice,
    expert_choice,
    running_counts,
    cotangent,
):
    seq_rows, model_width = tokens.shape
    groups = lax.axis_size("expert")
    grid = Grid(groups)
    me = lax.axis_index("expert")
    local_experts, _, ff = expert_up.shape
    experts_all = local_experts * groups
    picks_per = expert_choice.shape[1]
    cap = 3 * seq_rows * picks_per // (2 * experts_all)
    score_scale = 1.0 / math.sqrt(HEAD)
    position = jnp.arange(seq_rows, dtype=jnp.int32)
    seq_length = lengths[0]

    tree = Tree(lax.axis_size("dp"), grid)
    coords = tree.coords()
    code = jnp.where((position < seq_length)[:, None], expert_choice + 1, 0)
    digits = jnp.concatenate([code // 16, code % 16], axis=1).astype(BF)
    digits = digits.reshape(-1, model_width)
    meta_rows = digits.shape[0]
    meta = jnp.pad(digits, ((0, -meta_rows % 16), (0, 0)))
    grads_all = grid.all_rows(jnp.concatenate([cotangent, meta], axis=0))
    codes = jnp.stack([g[seq_rows : seq_rows + meta_rows] for g in grads_all])
    codes = codes.reshape(groups, seq_rows, 2, picks_per).astype(F32)
    picks = (codes[:, :, 0] * 16.0 + codes[:, :, 1]).astype(jnp.int32) - 1
    mine = me * local_experts + jnp.arange(local_experts, dtype=jnp.int32)
    member = jnp.any(picks[:, :, None, :] == mine[None, None, :, None], axis=3)
    below = (position[:, None] > position[None, :]).astype(BF)
    earlier = jnp.einsum("tu,sue->ste", below, member.astype(BF), preferred_element_type=F32)
    slot = jnp.where(member, earlier, -1.0)
    slot_low = slot.astype(BF)
    slot_t = jnp.swapaxes(slot, 1, 2)
    slots = [slot_t[s] for s in range(groups)]
    gs = [
        gather_call(grads_all[s : s + 2], slots[s : s + 2], cap) for s in range(0, groups, 2)
    ]

    inputs = tokens.astype(jnp.float32)
    row_mean = jnp.mean(inputs, axis=1, keepdims=True)
    centered = inputs - row_mean
    inverse_std = lax.rsqrt(jnp.mean(centered * centered, axis=1, keepdims=True) + 1e-05)
    scaled = centered * inverse_std
    normed_low = (scaled * norm_gain).astype(jnp.bfloat16)
    cosine, sine = rope_tables(seq_rows, HEAD)
    query_pre = jnp.dot(normed_low, query_weight, preferred_element_type=jnp.float32).reshape(
        seq_rows, HEADS, HEAD
    )
    key_pre = jnp.dot(normed_low, key_weight, preferred_element_type=jnp.float32).reshape(
        seq_rows, HEADS, HEAD
    )
    query_rot = rotate(query_pre, cosine, sine).astype(jnp.bfloat16)
    key_rot = rotate(key_pre, cosine, sine).astype(jnp.bfloat16)
    values_all = jnp.dot(tokens, value_weight, preferred_element_type=jnp.float32).reshape(
        seq_rows, HEADS, AEXP, HEAD
    )
    labels = jnp.arange(AEXP, dtype=jnp.int32)
    value_mask = jnp.sum((value_choice[..., None] == labels).astype(jnp.float32), axis=2)
    output_mask = jnp.sum((output_choice[..., None] == labels).astype(jnp.float32), axis=2)
    value_sig = jax.nn.sigmoid(
        jnp.dot(tokens, value_router, preferred_element_type=jnp.float32).reshape(
            seq_rows, HEADS, AEXP
        )
    )
    output_sig = jax.nn.sigmoid(
        jnp.dot(tokens, output_router, preferred_element_type=jnp.float32).reshape(
            seq_rows, HEADS, AEXP
        )
    )
    value_gate = value_sig * value_mask
    output_gate = output_sig * output_mask
    mixed = jnp.sum(value_gate[..., None] * values_all, axis=2).astype(jnp.bfloat16)

    allowed = (position[None, :] <= position[:, None]) & (position[None, :] < seq_length)
    scores = (
        jnp.einsum("qhw,khw->hqk", query_rot, key_rot, preferred_element_type=jnp.float32)
        * score_scale
    )
    scores = jnp.where(allowed[None], scores, -1e30)
    top = jnp.max(scores, axis=2, keepdims=True)
    expo = jnp.exp(scores - top)
    probs = expo / jnp.sum(expo, axis=2, keepdims=True)
    probs_low = probs.astype(jnp.bfloat16)
    attended = jnp.einsum("hqk,khw->qhw", probs_low, mixed, preferred_element_type=jnp.float32)
    expanded = (
        (output_gate[..., None] * attended[:, :, None, :])
        .astype(jnp.bfloat16)
        .reshape(seq_rows, HEADS * AEXP * HEAD)
    )
    hidden = inputs + contract_cols(expanded, output_weight)
    hidden_low = hidden.astype(jnp.bfloat16)

    hidden_all = grid.all_rows(hidden_low)
    xs = [
        gather_call(hidden_all[s : s + 2], slots[s : s + 2], cap) for s in range(0, groups, 2)
    ]
    router_mine = lax.dynamic_slice_in_dim(expert_router, me * local_experts, local_experts, 1)
    router_pad = jnp.pad(router_mine, ((0, 0), (0, ff - local_experts)))
    moe_parts, dhid_parts, near, far, grad_router_t = expert_call(
        coords, tree.xs, xs, gs, expert_up, expert_down, router_pad, slot_low, cap
    )
    dhidden = cotangent.astype(F32) + grid.sum_rows(dhid_parts).astype(F32)
    output = (hidden + grid.sum_rows(moe_parts).astype(F32)).astype(BF)
    got = tree.core_shift(far)
    acc, last = tree.ring_but_last(
        [add(near[i], got[i]) for i in range(tree.xs)], tree.x_shift
    )
    expert_grads = jnp.swapaxes(acc.astype(F32) + last.astype(F32), 2, 3)

    devices = tree.dp * groups
    rows_each = model_width // devices
    labels_all = jnp.arange(experts_all, dtype=jnp.int32)
    local_counts = jnp.sum(
        (code[:, :, None] == labels_all + 1).astype(jnp.int32), axis=(0, 1), dtype=jnp.int32
    )
    bits = (local_counts[:, None] >> jnp.arange(6, dtype=jnp.int32)) & 1
    bits = bits.reshape(devices, experts_all // devices, 6)
    bits = jnp.pad(bits, ((0, 0), (0, rows_each - experts_all // devices), (0, 0)))
    bits = bits.reshape(model_width, 6).astype(BF)
    routers = 2 * HEADS * AEXP
    small = -(-(routers + experts_all + 6) // 256) * 256
    extra = jnp.pad(bits, ((0, 0), (routers + experts_all, small - routers - experts_all - 6)))
    extra = lax.dynamic_update_slice_in_dim(
        extra,
        jnp.transpose(grad_router_t)[:, :local_experts].astype(BF),
        routers + me * local_experts,
        1,
    )

    dbranch_low = dhidden.astype(jnp.bfloat16)
    sum_output = tree.sum_rows(*spread_call(coords, tree, dbranch_low, expanded, 512))
    dexpanded = jnp.dot(dbranch_low, output_weight, preferred_element_type=jnp.float32).reshape(
        seq_rows, HEADS, AEXP, HEAD
    )
    dattended_low = jnp.sum(output_gate[..., None] * dexpanded, axis=2).astype(jnp.bfloat16)
    doutput_gate = jnp.sum(dexpanded * attended[:, :, None, :], axis=3)
    doutput_logit = (
        (doutput_gate * output_mask * output_sig * (1.0 - output_sig))
        .astype(jnp.bfloat16)
        .reshape(seq_rows, HEADS * AEXP)
    )
    dprobs = jnp.einsum("qhw,khw->hqk", dattended_low, mixed, preferred_element_type=jnp.float32)
    inner = jnp.sum(probs * dprobs, axis=2, keepdims=True)
    dscore_low = (probs * (dprobs - inner)).astype(jnp.bfloat16)
    dquery_rot = (
        jnp.einsum("hqk,khw->qhw", dscore_low, key_rot, preferred_element_type=jnp.float32)
        * score_scale
    )
    dkey_rot = (
        jnp.einsum("hqk,qhw->khw", dscore_low, query_rot, preferred_element_type=jnp.float32)
        * score_scale
    )
    dmixed = jnp.einsum(
        "hqk,qhw->khw", probs_low, dattended_low, preferred_element_type=jnp.float32
    )
    dquery_low = (
        unrotate(dquery_rot, cosine, sine).astype(jnp.bfloat16).reshape(seq_rows, HEADS * HEAD)
    )
    dkey_low = unrotate(dkey_rot, cosine, sine).astype(jnp.bfloat16).reshape(seq_rows, HEADS * HEAD)
    dvalues_low = (
        (value_gate[..., None] * dmixed[:, :, None, :])
        .astype(jnp.bfloat16)
        .reshape(seq_rows, HEADS * AEXP * HEAD)
    )
    dvalue_gate = jnp.sum(dmixed[:, :, None, :] * values_all, axis=3)
    dvalue_logit = (
        (dvalue_gate * value_mask * value_sig * (1.0 - value_sig))
        .astype(jnp.bfloat16)
        .reshape(seq_rows, HEADS * AEXP)
    )
    sum_value = tree.sum_rows(*spread_call(coords, tree, tokens, dvalues_low, 512))
    dqk_low = jnp.concatenate([dquery_low, dkey_low], axis=1)
    sum_qk = tree.sum_rows(*spread_call(coords, tree, normed_low, dqk_low, 512))
    dlogits = jnp.concatenate([dvalue_logit, doutput_logit], axis=1)
    dlogits = jnp.pad(dlogits, ((0, 0), (0, small - routers)))
    sum_small = tree.sum_rows(*spread_call(coords, tree, tokens, dlogits, small, extra))
    dnormed = contract_cols(dquery_low, query_weight) + contract_cols(dkey_low, key_weight)
    dscaled = dnormed * norm_gain
    dnorm_in = inverse_std * (
        dscaled
        - jnp.mean(dscaled, axis=1, keepdims=True)
        - scaled * jnp.mean(dscaled * scaled, axis=1, keepdims=True)
    )
    dinput_rest = (
        contract_cols(dvalues_low, value_weight)
        + contract_cols(dvalue_logit, value_router)
        + contract_cols(doutput_logit, output_router)
    )
    grad_tokens = (dhidden + dnorm_in + dinput_rest).astype(jnp.bfloat16)

    qk = HEADS * HEAD
    grad_query, grad_key = sum_qk[:, :qk], sum_qk[:, qk:]
    first = (lax.axis_index("dp") * groups + me) * rows_each
    rows_of = lambda w: lax.dynamic_slice_in_dim(w, first, rows_each, 0)
    grad_gain = jnp.sum(
        grad_query * rows_of(query_weight).astype(F32) + grad_key * rows_of(key_weight).astype(F32),
        axis=1,
    ) / rows_of(norm_gain)
    half = HEADS * AEXP
    got_bits = sum_small[: experts_all // devices, routers + experts_all :][:, :6]
    got_counts = jnp.sum(got_bits * (2.0 ** jnp.arange(6, dtype=F32)), axis=1)
    counts = running_counts + got_counts.astype(jnp.int32)
    return (
        output,
        grad_tokens,
        grad_gain,
        grad_query,
        grad_key,
        sum_value,
        sum_output,
        sum_small[:, :half],
        sum_small[:, half:routers],
        sum_small[:, routers : routers + experts_all],
        expert_grads[:, 0],
        expert_grads[:, 1],
        counts,
    )


def solution(mesh):
    both = ("dp", "expert")
    in_specs = (
        P(both, None),
        P(),
        P(),
        P(),
        P(),
        P(),
        P(),
        P(),
        P(),
        P("expert", None, None),
        P("expert", None, None),
        P(both),
        P(both, None, None),
        P(both, None, None),
        P(both, None),
        P(both),
        P(both, None),
    )
    out_specs = (
        P(both, None),
        P(both, None),
        P(both),
        P(both, None),
        P(both, None),
        P(both, None),
        P(both, None),
        P(both, None),
        P(both, None),
        P(both, None),
        P("expert", "dp", None),
        P("expert", "dp", None),
        P(both),
    )
    return jax.shard_map(shards, mesh=mesh, in_specs=in_specs, out_specs=out_specs, check_vma=False)
```

time: 2560 us -> 531 us (0.21)
  waiting for transfers between devices: 1470 us -> 251 us
  blocking collectives: 639 us -> 0 us
  local copies, waits for them, and re-layouts: 261 us -> 48.2 us
  Pallas kernels: 0 us -> 75.5 us
  matrix products: 119 us -> 45.2 us
  starting transfers between devices: 12.3 us -> 41.7 us
    reduce_scatter x6 -> x0, waiting for transfers between devices: 635 us -> none  [the longest x1 227 us: shards(): lax.psum_scatter(grad_output, ('dp', 'expert'), scatter_dimension=0, tile...]
    all_to_all x2 -> x0, blocking collectives: 559 us -> none  [the longest x1 282 us: shards(): lax.all_to_all(send_rows, 'expert', split_axis=0, concat_axis=0, tiled=True)]
    all_to_all x2 -> x0, waiting for transfers between devices: 490 us -> none  [the longest x1 252 us: shards(): lax.all_to_all(drows_expert, 'expert', split_axis=0, concat_axis=0, tiled...]
    unnamed x12 -> x0, waiting for transfers between devices: 349 us -> none
    ppermute x0 -> x54, waiting for transfers between devices: none -> 251 us  [the longest x20 125 us: lo_shift(): return lax.ppermute(x, 'expert', pairs)]
    gather x12 -> x0, local copies, waits for them, and re-layouts: 182 us -> none  [the longest x1 35.1 us: shards(): dpadded[owner].reshape(groups, local_experts, capacity, model_width)]
    dot_general x22 -> x6, matrix products: 93.5 us -> 8.07 us  [the longest x1 2.8 us: shards(): jnp.einsum('hqk,khw->qhw', probs_low, mixed, preferred_element_type=jnp.f...]
    unnamed x2 -> x0, blocking collectives: 79.6 us -> none
  transfers between devices with their start and end apart: 11 -> 54, of which waited for: 8 -> 35; matrix products, arithmetic and copies ran while one was open for 6% -> 22% of each run, Pallas kernels for 0% -> 2%
where the time goes in v1:
time: 531 us; the launch traced here: 521 us
  waiting for transfers between devices  251 us (47%)
  Pallas kernels  75.5 us (14%)
  other arithmetic  56 us (11%)
  local copies, waits for them, and re-layouts  48.2 us (9%)
  matrix products  45.2 us (9%)
  starting transfers between devices  41.7 us (8%)
    ppermute x20, waiting for transfers between devices, lo_shift(): return lax.ppermute(x, 'expert', pairs)  125 us
    ppermute x5, waiting for transfers between devices, x_shift(): return lax.ppermute(x, 'dp', pairs)  83.5 us
    pallas_call x1, Pallas kernels, expert_call(): pl.pallas_call(functools.partial(expert_kernel, groups, per, cap), grid_s...  47.7 us
    ppermute x24, waiting for transfers between devices, hi_shift(): return lax.ppermute(x, 'expert', pairs)  43.2 us
    unnamed x174, local copies, waits for them, and re-layouts  26.5 us
    ppermute x20, starting transfers between devices, lo_shift(): return lax.ppermute(x, 'expert', pairs)  24.4 us
    convert_element_type x27, other arithmetic, add(): return (a.astype(F32) + b.astype(F32)).astype(BF)  24.1 us
    dot_general x6, matrix products, contract_cols(): lax.dot_general(left, right, (((1,), (1,)), ((), ())), preferred_element_...  17.5 us
  transfers between devices with their start and end apart: 54, of which 35 were waited for; matrix products, arithmetic and copies ran while one was open for 22% of the time, Pallas kernels for 2%

profile of v1, /device:TPU:0, one launch (start us, length us, event | category | flops | bytes accessed | tf_op | source)
XLA Modules:
  0.0 521.2 jit_solution(12451557152752189837)
XLA Ops:
  10.1 6.3 %fusion.86 = f32[256,2560]{0,1:T(8,128)} fusion(bf16[256,1024]{1,0:T(8,128)(2,1)} %refs_0_.3, bf16[1024,2560]{1,0:T(8,128)(2,1)} %param.21), kind=kOutput, calls=%fused_computation.256 | convolution fusion | flops 1342177280 | bytes 8388608 | tf_op jit(solution)/shard_map/dot_general | solution.py:438
  39.7 5.6 %fusion.85 = (bf16[256,1024]{1,0:T(8,128)(2,1)S(1)}, f32[256,1024]{1,0:T(8,128)}) fusion(bf16[256,2560]{0,1:T(8,128)(2,1)S(1)} %bitcast.246, bf16[1024,2560]{1,0:T(8,128)(2,1)} %param.22, bf16[256,1024]{1,0:T(8,128)(2,1)S(1)} %copy-done.2), kind=kOutput, calls=%fused_computation.255 | convolution fusion | flops 1342963712 | bytes 8650752 | tf_op jit(solution)/shard_map/dot_general | solution.py:58
  51.3 8.9 %collective-permute-done.refs_1_ = bf16[256,1024]{1,0:T(8,128)(2,1)S(1)} collective-permute-done((bf16[256,1024]{1,0:T(8,128)(2,1)S(1)}, bf16[256,1024]{1,0:T(8,128)(2,1)S(1)}, u32[]{:S(2)}, u32[]{:S(2)}) %collective-permute-start) | collective-permute-done | bytes 524320 | tf_op jit(solution)/shard_map/ppermute | solution.py:79
  64.1 17.6 %collective-permute-done.9.refs_1_ = bf16[256,1024]{1,0:T(8,128)(2,1)} collective-permute-done((bf16[256,1024]{1,0:T(8,128)(2,1)}, bf16[256,1024]{1,0:T(8,128)(2,1)}, u32[]{:S(2)}, u32[]{:S(2)}) %collective-permute-start.9) | collective-permute-done | bytes 524320 | tf_op jit(solution)/shard_map/ppermute | solution.py:79
  89.4 9.5 %collective-permute-done.11.refs_1_ = bf16[256,1024]{1,0:T(8,128)(2,1)} collective-permute-done((bf16[256,1024]{1,0:T(8,128)(2,1)}, bf16[256,1024]{1,0:T(8,128)(2,1)}, u32[]{:S(2)}, u32[]{:S(2)}) %collective-permute-start.11) | collective-permute-done | bytes 524320 | tf_op jit(solution)/shard_map/ppermute | solution.py:79
  102.7 8.1 %collective-permute-done.6.refs_1_ = bf16[272,1024]{1,0:T(8,128)(2,1)} collective-permute-done((bf16[272,1024]{1,0:T(8,128)(2,1)}, bf16[272,1024]{1,0:T(8,128)(2,1)}, u32[]{:S(2)}, u32[]{:S(2)}) %collective-permute-start.6) | collective-permute-done | bytes 557088 | tf_op jit(solution)/shard_map/ppermute | solution.py:79
  116.2 5.9 %collective-permute-done.13.refs_1_ = bf16[256,1024]{1,0:T(8,128)(2,1)} collective-permute-done((bf16[256,1024]{1,0:T(8,128)(2,1)}, bf16[256,1024]{1,0:T(8,128)(2,1)}, u32[]{:S(2)}, u32[]{:S(2)}) %collective-permute-start.13) | collective-permute-done | bytes 524320 | tf_op jit(solution)/shard_map/ppermute | solution.py:79
  122.0 9.0 %collective-permute-done.8.refs_1_ = bf16[272,1024]{1,0:T(8,128)(2,1)} collective-permute-done((bf16[272,1024]{1,0:T(8,128)(2,1)}, bf16[272,1024]{1,0:T(8,128)(2,1)}, u32[]{:S(2)}, u32[]{:S(2)}) %collective-permute-start.8) | collective-permute-done | bytes 557088 | tf_op jit(solution)/shard_map/ppermute | solution.py:79
  165.2 47.7 %experts.1 = (bf16[256,1024]{1,0:T(8,128)(2,1)}, bf16[256,1024]{1,0:T(8,128)(2,1)}, bf16[256,1024]{1,0:T(8,128)(2,1)}, bf16[256,1024]{1,0:T(8,128)(2,1)}, bf16[2...) custom-call(s32[4]{0:T(128)} %pad_add_fusion.at_ref, ...), custom_call_target="tpu_custom_call" | custom-call | flops 19327352832 | bytes 50331648 | tf_op jit(solution)/shard_map/experts/pallas_call | solution.py:283
  216.6 11.5 %collective-permute-done.24 = bf16[256,1024]{1,0:T(8,128)(2,1)S(1)} collective-permute-done((bf16[256,1024]{1,0:T(8,128)(2,1)}, bf16[256,1024]{1,0:T(8,128)(2,1)S(1)}, u32[]{:S(2)}, u32[]{:S(2)}) %collective-permute-start.24) | collective-permute-done | bytes 524320 | tf_op jit(solution)/shard_map/ppermute | solution.py:79
  233.8 5.7 %collective-permute-done.17 = bf16[256,1024]{1,0:T(8,128)(2,1)} collective-permute-done((bf16[256,1024]{1,0:T(8,128)(2,1)}, bf16[256,1024]{1,0:T(8,128)(2,1)}, u32[]{:S(2)}, u32[]{:S(2)}) %collective-permute-start.17) | collective-permute-done | bytes 524320 | tf_op jit(solution)/shard_map/ppermute | solution.py:79
  240.8 9.9 %collective-permute-done.23 = bf16[256,1024]{1,0:T(8,128)(2,1)} collective-permute-done((bf16[256,1024]{1,0:T(8,128)(2,1)}, bf16[256,1024]{1,0:T(8,128)(2,1)}, u32[]{:S(2)}, u32[]{:S(2)}) %collective-permute-start.23) | collective-permute-done | bytes 524320 | tf_op jit(solution)/shard_map/ppermute | solution.py:79
  255.3 6.6 %collective-permute-done.16 = bf16[256,1024]{1,0:T(8,128)(2,1)} collective-permute-done((bf16[256,1024]{1,0:T(8,128)(2,1)}, bf16[256,1024]{1,0:T(8,128)(2,1)}, u32[]{:S(2)}, u32[]{:S(2)}) %collective-permute-start.16) | collective-permute-done | bytes 524320 | tf_op jit(solution)/shard_map/ppermute | solution.py:79
  265.8 7.4 %collective-permute-done.22 = bf16[256,1024]{1,0:T(8,128)(2,1)} collective-permute-done((bf16[256,1024]{1,0:T(8,128)(2,1)}, bf16[256,1024]{1,0:T(8,128)(2,1)}, u32[]{:S(2)}, u32[]{:S(2)}) %collective-permute-start.22) | collective-permute-done | bytes 524320 | tf_op jit(solution)/shard_map/ppermute | solution.py:79
  286.9 8.7 %collective-permute-done.21 = bf16[256,1024]{1,0:T(8,128)(2,1)S(1)} collective-permute-done((bf16[256,1024]{1,0:T(8,128)(2,1)}, bf16[256,1024]{1,0:T(8,128)(2,1)S(1)}, u32[]{:S(2)}, u32[]{:S(2)}) %collective-permute-start.21) | collective-permute-done | bytes 524320 | tf_op jit(solution)/shard_map/ppermute | solution.py:79
  297.2 4.9 fusion.89
  354.5 8.7 %collective-permute-done.29 = bf16[2,4,32,1024]{3,2,1,0:T(8,128)(2,1)S(1)} collective-permute-done((bf16[2,4,32,1024]{3,2,1,0:T(8,128)(2,1)S(1)}, bf16[2,4,32,1024]{3,2,1,0:T(8,128)(2,1)S(1)}, u32[]{:S(2)}, u32[]{:S(2)}) %collective-permute-start.29) | collective-permute-done | bytes 524320 | tf_op jit(solution)/shard_map/ppermute | solution.py:140
  364.3 6.4 %collective-permute-done.30 = bf16[4,32,1024]{2,1,0:T(8,128)(2,1)S(1)} collective-permute-done((bf16[4,32,1024]{2,1,0:T(8,128)(2,1)S(1)}, bf16[4,32,1024]{2,1,0:T(8,128)(2,1)S(1)}, u32[]{:S(2)}, u32[]{:S(2)}) %collective-permute-start.30) | collective-permute-done | bytes 262176 | tf_op jit(solution)/shard_map/ppermute | solution.py:79
  371.4 5.5 %collective-permute-done.31 = bf16[32,1024]{1,0:T(8,128)(2,1)S(1)} collective-permute-done((bf16[32,1024]{1,0:T(8,128)(2,1)S(1)}, bf16[32,1024]{1,0:T(8,128)(2,1)S(1)}, u32[]{:S(2)}, u32[]{:S(2)}) %collective-permute-start.31) | collective-permute-done | bytes 65568 | tf_op jit(solution)/shard_map/ppermute | solution.py:73
  395.4 21.2 %collective-permute-done.35 = bf16[2,4,32,2560]{3,2,1,0:T(8,128)(2,1)S(1)} collective-permute-done((bf16[2,4,32,2560]{3,2,1,0:T(8,128)(2,1)S(1)}, bf16[2,4,32,2560]{3,2,1,0:T(8,128)(2,1)S(1)}, u32[]{:S(2)}, u32[]{:S(2)}) %collective-permute-start.35) | collective-permute-done | bytes 1310752 | tf_op jit(solution)/shard_map/ppermute | solution.py:140
  419.0 20.2 %collective-permute-done.41 = bf16[2,4,32,2560]{3,2,1,0:T(8,128)(2,1)S(1)} collective-permute-done((bf16[2,4,32,2560]{3,2,1,0:T(8,128)(2,1)S(1)}, bf16[2,4,32,2560]{3,2,1,0:T(8,128)(2,1)S(1)}, u32[]{:S(2)}, u32[]{:S(2)}) %collective-permute-start.41) | collective-permute-done | bytes 1310752 | tf_op jit(solution)/shard_map/ppermute | solution.py:140
  446.9 5.6 %collective-permute-done.42 = bf16[4,32,2560]{2,1,0:T(8,128)(2,1)S(1)} collective-permute-done((bf16[4,32,2560]{2,1,0:T(8,128)(2,1)S(1)}, bf16[4,32,2560]{2,1,0:T(8,128)(2,1)S(1)}, u32[]{:S(2)}, u32[]{:S(2)}) %collective-permute-start.42) | collective-permute-done | bytes 655392 | tf_op jit(solution)/shard_map/ppermute | solution.py:79
  455.6 6.0 %collective-permute-done.43 = bf16[32,2560]{1,0:T(8,128)(2,1)S(1)} collective-permute-done((bf16[32,2560]{1,0:T(8,128)(2,1)S(1)}, bf16[32,2560]{1,0:T(8,128)(2,1)S(1)}, u32[]{:S(2)}, u32[]{:S(2)}) %collective-permute-start.43) | collective-permute-done | bytes 163872 | tf_op jit(solution)/shard_map/ppermute | solution.py:73
  477.9 31.4 %collective-permute-done.53 = bf16[24,2,128,256]{3,2,1,0:T(8,128)(2,1)S(1)} collective-permute-done((bf16[24,2,128,256]{3,2,1,0:T(8,128)(2,1)S(1)}, bf16[24,2,128,256]{3,2,1,0:T(8,128)(2,1)S(1)}, u32[]{:S(2)}, u32[]{:S(2)}) %collective-permute-start.53) | collective-permute-done | bytes 3145760 | tf_op jit(solution)/shard_map/ppermute | solution.py:140
  (435 shorter events, 239.8 us)
Async XLA Ops:
  3.5 44.7 %collective-permute-start.2 = (bf16[272,1024]{1,0:T(8,128)(2,1)S(1)}, bf16[272,1024]{1,0:T(8,128)(2,1)S(1)}, u32[]{:S(2)}, u32[]{:S(2)}) collective-permute-start(bf16[272,1024]{1,0:T(8,128)(2,1)S(1)} %fusion.41.refs_0_), channel_id=1, source_target_pairs={{0,1},{1,0},{2,3},{3,2},{4,5},{5,4},{6,7},{7,6},{8,9},{9,8},{10,11... | collective-permute-start | bytes 1671176 | tf_op jit(solution)/shard_map/ppermute | solution.py:79
  6.5 41.6 %collective-permute-start.3 = (bf16[272,1024]{1,0:T(8,128)(2,1)S(1)}, bf16[272,1024]{1,0:T(8,128)(2,1)S(1)}, u32[]{:S(2)}, u32[]{:S(2)}) collective-permute-start(bf16[272,1024]{1,0:T(8,128)(2,1)S(1)} %fusion.41.refs_0_), channel_id=1, source_target_pairs={{0,2},{1,3},{2,4},{3,5},{4,6},{5,7},{6,0},{7,1},{8,10},{9,11},{10,... | collective-permute-start | bytes 1671176 | tf_op jit(solution)/shard_map/ppermute | solution.py:73
  48.2 37.0 %collective-permute-start.4 = (bf16[272,1024]{1,0:T(8,128)(2,1)S(1)}, bf16[272,1024]{1,0:T(8,128)(2,1)}, u32[]{:S(2)}, u32[]{:S(2)}) collective-permute-start(bf16[272,1024]{1,0:T(8,128)(2,1)S(1)} %collective-permute-done.3.refs_0_), channel_id=1, source_target_pairs={{0,1},{1,0},{2,3},{3,2},{4,5},{5,4},{6,7},{7,6},{8,9},{9,8},{10,11... | collective-permute-start | bytes 1671176 | tf_op jit(solution)/shard_map/ppermute | solution.py:79
  49.7 35.5 %collective-permute-start.5 = (bf16[272,1024]{1,0:T(8,128)(2,1)S(1)}, bf16[272,1024]{1,0:T(8,128)(2,1)}, u32[]{:S(2)}, u32[]{:S(2)}) collective-permute-start(bf16[272,1024]{1,0:T(8,128)(2,1)S(1)} %collective-permute-done.3.refs_0_), channel_id=1, source_target_pairs={{0,2},{1,3},{2,4},{3,5},{4,6},{5,7},{6,0},{7,1},{8,10},{9,11},{10,... | collective-permute-start | bytes 1671176 | tf_op jit(solution)/shard_map/ppermute | solution.py:73
  85.2 25.6 %collective-permute-start.6 = (bf16[272,1024]{1,0:T(8,128)(2,1)}, bf16[272,1024]{1,0:T(8,128)(2,1)}, u32[]{:S(2)}, u32[]{:S(2)}) collective-permute-start(bf16[272,1024]{1,0:T(8,128)(2,1)} %collective-permute-done.5.refs_0_), channel_id=1, source_target_pairs={{0,1},{1,0},{2,3},{3,2},{4,5},{5,4},{6,7},{7,6},{8,9},{9,8},{10,11... | collective-permute-start | bytes 1671176 | tf_op jit(solution)/shard_map/ppermute | solution.py:79
  85.8 25.1 %collective-permute-start.7 = (bf16[272,1024]{1,0:T(8,128)(2,1)}, bf16[272,1024]{1,0:T(8,128)(2,1)}, u32[]{:S(2)}, u32[]{:S(2)}) collective-permute-start(bf16[272,1024]{1,0:T(8,128)(2,1)} %collective-permute-done.5.refs_0_), channel_id=1, source_target_pairs={{0,2},{1,3},{2,4},{3,5},{4,6},{5,7},{6,0},{7,1},{8,10},{9,11},{10,... | collective-permute-start | bytes 1671176 | tf_op jit(solution)/shard_map/ppermute | solution.py:73
  110.9 20.1 %collective-permute-start.8 = (bf16[272,1024]{1,0:T(8,128)(2,1)}, bf16[272,1024]{1,0:T(8,128)(2,1)}, u32[]{:S(2)}, u32[]{:S(2)}) collective-permute-start(bf16[272,1024]{1,0:T(8,128)(2,1)} %collective-permute-done.7.refs_0_), channel_id=1, source_target_pairs={{0,1},{1,0},{2,3},{3,2},{4,5},{5,4},{6,7},{7,6},{8,9},{9,8},{10,11... | collective-permute-start | bytes 1671176 | tf_op jit(solution)/shard_map/ppermute | solution.py:79
  214.6 24.9 %collective-permute-start.17 = (bf16[256,1024]{1,0:T(8,128)(2,1)}, bf16[256,1024]{1,0:T(8,128)(2,1)}, u32[]{:S(2)}, u32[]{:S(2)}) collective-permute-start(bf16[256,1024]{1,0:T(8,128)(2,1)} %get-tuple-element.71), channel_id=1, source_target_pairs={{0,1},{1,0},{2,3},{3,2},{4,5},{5,4},{6,7},{7,6},{8,9},{9,8},{10,11... | collective-permute-start | bytes 1572872 | tf_op jit(solution)/shard_map/ppermute | solution.py:79
  215.1 35.6 %collective-permute-start.23 = (bf16[256,1024]{1,0:T(8,128)(2,1)}, bf16[256,1024]{1,0:T(8,128)(2,1)}, u32[]{:S(2)}, u32[]{:S(2)}) collective-permute-start(bf16[256,1024]{1,0:T(8,128)(2,1)} %get-tuple-element.77), channel_id=1, source_target_pairs={{0,1},{1,0},{2,3},{3,2},{4,5},{5,4},{6,7},{7,6},{8,9},{9,8},{10,11... | collective-permute-start | bytes 1572872 | tf_op jit(solution)/shard_map/ppermute | solution.py:79
  230.2 20.5 %collective-permute-start.25 = (bf16[256,1024]{1,0:T(8,128)(2,1)}, bf16[256,1024]{1,0:T(8,128)(2,1)}, u32[]{:S(2)}, u32[]{:S(2)}) collective-permute-start(bf16[256,1024]{1,0:T(8,128)(2,1)} %add_convert_fusion.11), channel_id=1, source_target_pairs={{0,2},{1,3},{2,4},{3,5},{4,6},{5,7},{6,0},{7,1},{8,10},{9,11},{10,... | collective-permute-start | bytes 1572872 | tf_op jit(solution)/shard_map/ppermute | solution.py:73
  231.7 30.2 %collective-permute-start.16 = (bf16[256,1024]{1,0:T(8,128)(2,1)}, bf16[256,1024]{1,0:T(8,128)(2,1)}, u32[]{:S(2)}, u32[]{:S(2)}) collective-permute-start(bf16[256,1024]{1,0:T(8,128)(2,1)} %get-tuple-element.69), channel_id=1, source_target_pairs={{0,1},{1,0},{2,3},{3,2},{4,5},{5,4},{6,7},{7,6},{8,9},{9,8},{10,11... | collective-permute-start | bytes 1572872 | tf_op jit(solution)/shard_map/ppermute | solution.py:79
  233.3 39.9 %collective-permute-start.22 = (bf16[256,1024]{1,0:T(8,128)(2,1)}, bf16[256,1024]{1,0:T(8,128)(2,1)}, u32[]{:S(2)}, u32[]{:S(2)}) collective-permute-start(bf16[256,1024]{1,0:T(8,128)(2,1)} %get-tuple-element.75), channel_id=1, source_target_pairs={{0,1},{1,0},{2,3},{3,2},{4,5},{5,4},{6,7},{7,6},{8,9},{9,8},{10,11... | collective-permute-start | bytes 1572872 | tf_op jit(solution)/shard_map/ppermute | solution.py:79
  240.8 22.7 %collective-permute-start.18 = (bf16[256,1024]{1,0:T(8,128)(2,1)S(1)}, bf16[256,1024]{1,0:T(8,128)(2,1)S(1)}, u32[]{:S(2)}, u32[]{:S(2)}) collective-permute-start(bf16[256,1024]{1,0:T(8,128)(2,1)S(1)} %add_convert_fusion.19), channel_id=1, source_target_pairs={{0,2},{1,3},{2,4},{3,5},{4,6},{5,7},{6,0},{7,1},{8,10},{9,11},{10,... | collective-permute-start | bytes 1572872 | tf_op jit(solution)/shard_map/ppermute | solution.py:73
  253.7 30.7 %collective-permute-start.15 = (bf16[256,1024]{1,0:T(8,128)(2,1)}, bf16[256,1024]{1,0:T(8,128)(2,1)}, u32[]{:S(2)}, u32[]{:S(2)}) collective-permute-start(bf16[256,1024]{1,0:T(8,128)(2,1)} %get-tuple-element.67), channel_id=1, source_target_pairs={{0,1},{1,0},{2,3},{3,2},{4,5},{5,4},{6,7},{7,6},{8,9},{9,8},{10,11... | collective-permute-start | bytes 1572872 | tf_op jit(solution)/shard_map/ppermute | solution.py:79
  261.9 33.6 %collective-permute-start.21 = (bf16[256,1024]{1,0:T(8,128)(2,1)}, bf16[256,1024]{1,0:T(8,128)(2,1)S(1)}, u32[]{:S(2)}, u32[]{:S(2)}) collective-permute-start(bf16[256,1024]{1,0:T(8,128)(2,1)} %get-tuple-element.73), channel_id=1, source_target_pairs={{0,1},{1,0},{2,3},{3,2},{4,5},{5,4},{6,7},{7,6},{8,9},{9,8},{10,11... | collective-permute-start | bytes 1572872 | tf_op jit(solution)/shard_map/ppermute | solution.py:79
  276.3 72.6 %collective-permute-start.14 = (bf16[256,1024]{1,0:T(8,128)(2,1)}, bf16[256,1024]{1,0:T(8,128)(2,1)}, u32[]{:S(2)}, u32[]{:S(2)}) collective-permute-start(bf16[256,1024]{1,0:T(8,128)(2,1)} %get-tuple-element.65), channel_id=1, source_target_pairs={{0,1},{1,0},{2,3},{3,2},{4,5},{5,4},{6,7},{7,6},{8,9},{9,8},{10,11... | collective-permute-start | bytes 1572872 | tf_op jit(solution)/shard_map/ppermute | solution.py:79
  284.4 157.3 %collective-permute-start.52 = (bf16[2,24,2,128,256]{4,3,2,1,0:T(8,128)(2,1)}, bf16[2,24,2,128,256]{4,3,2,1,0:T(8,128)(2,1)}, u32[]{:S(2)}, u32[]{:S(2)}) collective-permute-start(bf16[2,24,2,128,256]{4,3,2,1,0:T(8,128)(2,1)} %get-tuple-element.90), channel_id=1, source_target_pairs={{0,8},{8,0},{16,24},{24,16},{1,9},{9,1},{17,25},{25,17},{2,10},{10... | collective-permute-start | bytes 18874376 | tf_op jit(solution)/shard_map/ppermute | solution.py:136
  286.8 62.8 %collective-permute-start.20 = (bf16[256,1024]{1,0:T(8,128)(2,1)}, bf16[256,1024]{1,0:T(8,128)(2,1)}, u32[]{:S(2)}, u32[]{:S(2)}) collective-permute-start(bf16[256,1024]{1,0:T(8,128)(2,1)} %add_convert_fusion.17), channel_id=1, source_target_pairs={{0,2},{1,3},{2,4},{3,5},{4,6},{5,7},{6,0},{7,1},{8,10},{9,11},{10,... | collective-permute-start | bytes 1572872 | tf_op jit(solution)/shard_map/ppermute | solution.py:73
  348.1 35.1 %collective-permute-start.34 = (bf16[2,2,4,32,2560]{4,3,2,1,0:T(8,128)(2,1)}, bf16[2,2,4,32,2560]{4,3,2,1,0:T(8,128)(2,1)}, u32[]{:S(2)}, u32[]{:S(2)}) collective-permute-start(bf16[2,2,4,32,2560]{4,3,2,1,0:T(8,128)(2,1)} %get-tuple-element.83), channel_id=1, source_target_pairs={{0,8},{8,0},{16,24},{24,16},{1,9},{9,1},{17,25},{25,17},{2,10},{10... | collective-permute-start | bytes 7864328 | tf_op jit(solution)/shard_map/ppermute | solution.py:136
  348.1 43.9 %collective-permute-start.40 = (bf16[2,2,4,32,2560]{4,3,2,1,0:T(8,128)(2,1)}, bf16[2,2,4,32,2560]{4,3,2,1,0:T(8,128)(2,1)}, u32[]{:S(2)}, u32[]{:S(2)}) collective-permute-start(bf16[2,2,4,32,2560]{4,3,2,1,0:T(8,128)(2,1)} %get-tuple-element.85), channel_id=1, source_target_pairs={{0,8},{8,0},{16,24},{24,16},{1,9},{9,1},{17,25},{25,17},{2,10},{10... | collective-permute-start | bytes 7864328 | tf_op jit(solution)/shard_map/ppermute | solution.py:136
  384.8 31.8 %collective-permute-start.35 = (bf16[2,4,32,2560]{3,2,1,0:T(8,128)(2,1)S(1)}, bf16[2,4,32,2560]{3,2,1,0:T(8,128)(2,1)S(1)}, u32[]{:S(2)}, u32[]{:S(2)}) collective-permute-start(bf16[2,4,32,2560]{3,2,1,0:T(8,128)(2,1)S(1)} %fusion.12), channel_id=1, source_target_pairs={{0,16},{8,24},{16,0},{24,8},{1,17},{9,25},{17,1},{25,9},{2,18},{10... | collective-permute-start | bytes 3932168 | tf_op jit(solution)/shard_map/ppermute | solution.py:140
  393.8 45.4 %collective-permute-start.41 = (bf16[2,4,32,2560]{3,2,1,0:T(8,128)(2,1)S(1)}, bf16[2,4,32,2560]{3,2,1,0:T(8,128)(2,1)S(1)}, u32[]{:S(2)}, u32[]{:S(2)}) collective-permute-start(bf16[2,4,32,2560]{3,2,1,0:T(8,128)(2,1)S(1)} %fusion.14), channel_id=1, source_target_pairs={{0,16},{8,24},{16,0},{24,8},{1,17},{9,25},{17,1},{25,9},{2,18},{10... | collective-permute-start | bytes 3932168 | tf_op jit(solution)/shard_map/ppermute | solution.py:140
  418.4 27.9 %collective-permute-start.36 = (bf16[4,32,2560]{2,1,0:T(8,128)(2,1)S(1)}, bf16[4,32,2560]{2,1,0:T(8,128)(2,1)S(1)}, u32[]{:S(2)}, u32[]{:S(2)}) collective-permute-start(bf16[4,32,2560]{2,1,0:T(8,128)(2,1)S(1)} %slice_bitcast_fusion.4), channel_id=1, source_target_pairs={{0,1},{1,0},{2,3},{3,2},{4,5},{5,4},{6,7},{7,6},{8,9},{9,8},{10,11... | collective-permute-start | bytes 1966088 | tf_op jit(solution)/shard_map/ppermute | solution.py:79
  444.8 64.5 %collective-permute-start.53 = (bf16[24,2,128,256]{3,2,1,0:T(8,128)(2,1)S(1)}, bf16[24,2,128,256]{3,2,1,0:T(8,128)(2,1)S(1)}, u32[]{:S(2)}, u32[]{:S(2)}) collective-permute-start(bf16[24,2,128,256]{3,2,1,0:T(8,128)(2,1)S(1)} %fusion.2), channel_id=1, source_target_pairs={{0,16},{8,24},{16,0},{24,8},{1,17},{9,25},{17,1},{25,9},{2,18},{10... | collective-permute-start | bytes 9437192 | tf_op jit(solution)/shard_map/ppermute | solution.py:140
  (110 other events, 1038.7 us)

commit v2 on v1

v2 whole, which is shorter than its diff:
```python
import functools
import math

import jax
import jax.numpy as jnp
from jax import lax
from jax.experimental import pallas as pl
from jax.experimental.pallas import tpu as pltpu
from jax.sharding import PartitionSpec as P

HEADS = 4
HEAD = 128
AEXP = 5
BF = jnp.bfloat16
F32 = jnp.float32
VMEM_LIMIT = 60 * 1024 * 1024
GELU_C = math.sqrt(2.0 / math.pi)
GELU_K = 0.044715


def rope_tables(seq_rows, head_width):
    half_width = head_width // 2
    ladder = jnp.arange(half_width, dtype=jnp.float32) * (2.0 / head_width)
    freqs = jnp.exp(-math.log(10000.0) * ladder)
    angles = jnp.arange(seq_rows, dtype=jnp.float32)[:, None] * freqs[None, :]
    cosine, sine = jnp.cos(angles), jnp.sin(angles)
    return (
        jnp.concatenate([cosine, cosine], axis=1),
        jnp.concatenate([-sine, sine], axis=1),
    )


class Task:
    def __init__(self, gen):
        self.gen = gen
        self.done = False
        self.result = None
        self.advance(None)

    def advance(self, value):
        try:
            self.out = self.gen.send(value)
        except StopIteration as stop:
            self.done, self.out, self.result = True, None, stop.value


def end_round(tasks, extra=()):
    tasks = [t for t in tasks if not t.done]
    got, extra = lax.optimization_barrier((tuple(t.out for t in tasks), extra))
    for task, value in zip(tasks, got):
        task.advance(value)
    return extra


def finish(tasks, extra=()):
    while any(not t.done for t in tasks):
        extra = end_round(tasks, extra)
    return extra


def total(*parts):
    return functools.reduce(lambda a, b: a + b, [p.astype(F32) for p in parts])


def add(*parts):
    return total(*parts).astype(BF)


class Grid:
    def __init__(self, dp, size):
        self.dp = dp
        self.xs = dp // 2
        self.hi = 4
        self.lo = size // 4
        self.size = size

    def coords(self):
        dp, ex = lax.axis_index("dp"), lax.axis_index("expert")
        return jnp.stack([dp % 2, dp // 2, ex % self.lo, ex // self.lo])

    def half(self, x, axis, core):
        shape = x.shape
        each = shape[axis] // self.dp
        x = x.reshape(shape[:axis] + (self.xs, 2, each) + shape[axis + 1 :])
        x = lax.dynamic_index_in_dim(x, core, axis + 1, False)
        return x.reshape(shape[:axis] + (self.xs * each,) + shape[axis + 1 :])

    def core_shift(self, x):
        return lax.ppermute(x, "dp", [(i, i ^ 1) for i in range(self.dp)])

    def x_shift(self, x):
        pairs = [(i, (i // 2 + 1) % self.xs * 2 + i % 2) for i in range(self.dp)]
        return lax.ppermute(x, "dp", pairs)

    def hi_shift(self, x, by=1):
        pairs = [
            (i, ((i // self.lo + by) % self.hi) * self.lo + i % self.lo) for i in range(self.size)
        ]
        return lax.ppermute(x, "expert", pairs)

    def lo_shift(self, x):
        pairs = [
            (i, (i // self.lo) * self.lo + (i % self.lo + 1) % self.lo) for i in range(self.size)
        ]
        return lax.ppermute(x, "expert", pairs)

    def sources(self):
        me = lax.axis_index("expert")
        h, l = me // self.lo, me % self.lo
        return [
            ((h + self.hi - dh) % self.hi) * self.lo + (l + self.lo - dl) % self.lo
            for dh in range(self.hi)
            for dl in range(self.lo)
        ]

    def gather_rows(self, block, known, last_over_hi=False):
        rows = {(0, 0): block}
        known[0] = block
        steps = self.hi + self.lo - 2
        last = (self.hi - 1, self.lo - 1)
        for step in range(steps):
            fresh = {}
            for dh in range(self.hi):
                for dl in range(self.lo):
                    if dh + dl == step + 1:
                        if dl == 0 or (last_over_hi and (dh, dl) == last):
                            fresh[(dh, dl)] = self.hi_shift(rows[(dh - 1, dl)])
                        else:
                            fresh[(dh, dl)] = self.lo_shift(rows[(dh, dl - 1)])
            got = yield fresh
            for (dh, dl), value in got.items():
                known[dh * self.lo + dl] = value
            if last_over_hi and step == steps - 2:
                got = yield got
            rows.update(got)

    def at(self, a, b):
        return ((self.hi - a) % self.hi) * self.lo + (self.lo - b) % self.lo

    def sum_rows(self, part):
        p = lambda a, b: part(self.at(a, b))
        sums = {}
        for step in range(self.hi + self.lo - 2):
            sent = {}
            for a in range(self.hi):
                for b in range(self.lo):
                    if (self.hi - 1 - a) + (self.lo - 1 - b) == step:
                        mine = add(p(a, b), *sums.pop((a, b), ()))
                        if b > 0:
                            sent[(a, b - 1, 0)] = self.lo_shift(mine)
                        else:
                            sent[(a - 1, b, 1)] = self.hi_shift(mine)
            got = yield sent
            for (a, b, _), value in got.items():
                sums.setdefault((a, b), []).append(value)
        return [p(0, 0), *sums.pop((0, 0))]

    def sum_rows_hi(self, part):
        p = lambda a, b: part(self.at(a, b))
        if self.lo != 2:
            return (yield from self.sum_rows(part))
        one, own = yield self.hi_shift(p(3, 1)), self.lo_shift(p(0, 1))
        one, two = yield self.lo_shift(add(p(2, 1), one)), self.hi_shift(p(3, 0))
        one, two = yield self.hi_shift(add(p(2, 0), one, two)), self.lo_shift(p(1, 1))
        one = yield self.hi_shift(add(p(1, 0), one, two))
        return [p(0, 0), own, one]

    def ring(self, parts, shift):
        acc = parts[-1]
        for b in range(len(parts) - 2, -1, -1):
            acc = yield shift(acc)
            if b:
                acc = add(parts[b], acc)
        return [parts[0], acc]

    def tree(self, parts, order):
        shifts = {"x": self.x_shift, "lo": self.lo_shift, "hi": self.hi_shift}
        left = ["x", "lo", "hi"]
        for name in order:
            if name != order[0]:
                axis = left.index(name)
                parts = [
                    add(*[lax.index_in_dim(v, i, axis, False) for v in acc])
                    for i in range(acc[0].shape[axis])
                ]
            left.remove(name)
            if name == order[-1] == "hi":
                acc = yield [self.hi_shift(parts[b], b) for b in range(1, self.hi)]
                return total(parts[0], *acc)
            acc = yield from self.ring(parts, shifts[name])
        return total(*acc)

    def expert_tree(self, near, far, cuts):
        got = yield self.core_shift(far)
        each = near.shape[1] // cuts
        out = []
        for c in range(cuts):
            cut = slice(c * each, (c + 1) * each)
            acc = add(near[self.xs - 1, cut], got[self.xs - 1, cut])
            for b in range(self.xs - 2, -1, -1):
                acc, near, got = yield self.x_shift(acc), near, got
                if b:
                    acc = add(near[b, cut], got[b, cut], acc)
            out.append((near[0, cut], got[0, cut], acc))
        return out


def gather_kernel(js, cap, *refs):
    count = len(js)
    rows, slots, out = refs[:count], [refs[count].at[j] for j in js], refs[count + 1]
    step, seq_rows = slots[0].shape
    for i in range(count):
        place = lax.broadcasted_iota(jnp.int32, (step, cap, seq_rows), 1).astype(F32)
        pick = (slots[i][...][:, None, :] == place).astype(F32).astype(BF)
        got = jnp.dot(
            pick.reshape(step * cap, seq_rows), rows[i][...], preferred_element_type=F32
        )
        out[:, i * cap : (i + 1) * cap, :] = got.astype(BF).reshape(step, cap, got.shape[1])


def slot_kernel(count, base_ref, *refs):
    codes, out, turned = refs[:count], refs[count], refs[count + 1]
    _, experts, seq_rows = out.shape
    ids = base_ref[0] + 1 + lax.broadcasted_iota(jnp.int32, (experts, seq_rows), 0)
    before = lax.broadcasted_iota(jnp.int32, (seq_rows, seq_rows), 0)
    after = lax.broadcasted_iota(jnp.int32, (seq_rows, seq_rows), 1)
    earlier = (before < after).astype(F32).astype(BF)
    for s in range(count):
        member = codes[s][0:1, :] == ids
        for k in range(1, codes[s].shape[0]):
            member = member | (codes[s][k : k + 1, :] == ids)
        ones = member.astype(F32)
        place = jnp.dot(ones.astype(BF), earlier, preferred_element_type=F32)
        slot = jnp.where(member, place, -1.0)
        out[s] = slot
        turned[s] = jnp.transpose(slot).astype(BF)


def slot_call(codes, base, experts):
    count = len(codes)
    seq_rows = codes[0].shape[1]
    vmem = pl.BlockSpec(memory_space=pltpu.VMEM)
    return pl.pallas_call(
        functools.partial(slot_kernel, count),
        in_specs=[pl.BlockSpec(memory_space=pltpu.SMEM)] + [vmem] * count,
        out_specs=[vmem, vmem],
        out_shape=[
            jax.ShapeDtypeStruct((count, experts, seq_rows), F32),
            jax.ShapeDtypeStruct((count, seq_rows, experts), BF),
        ],
        compiler_params=pltpu.CompilerParams(vmem_limit_bytes=20 * 1024 * 1024),
        name="slots",
    )(base, *codes)


def gather_call(rows, slots, js, cap):
    count = len(rows)
    experts = slots.shape[1]
    width = rows[0].shape[1]
    groups, _, seq_rows = slots.shape
    flops = 2 * count * experts * cap * seq_rows * width
    return pl.pallas_call(
        functools.partial(gather_kernel, js, cap),
        grid=(experts // 8,),
        in_specs=[pl.BlockSpec((seq_rows, width), lambda i: (0, 0))] * count
        + [pl.BlockSpec((groups, 8, seq_rows), lambda i: (0, i, 0))],
        out_specs=pl.BlockSpec((8, count * cap, width), lambda i: (i, 0, 0)),
        out_shape=jax.ShapeDtypeStruct((experts, count * cap, width), BF),
        compiler_params=pltpu.CompilerParams(vmem_limit_bytes=VMEM_LIMIT),
        cost_estimate=pl.CostEstimate(
            flops=flops, bytes_accessed=2 * experts * count * cap * width, transcendentals=0
        ),
        name="gather_rows",
    )(*rows, slots)


def expert_kernel(groups, per, cap, many, at_ref, *refs):
    n = groups // per
    xs_in, gs_in = refs[:n], refs[n : 2 * n]
    up, down, router = refs[2 * n : 2 * n + 3]
    outs = refs[2 * n + 3 :]
    moe = outs[:groups]
    dhid = outs[groups : 2 * groups]
    near, far, grt = outs[2 * groups : 2 * groups + 3]
    xs, gs, w, d2, gacc = outs[2 * groups + 3 :]
    step = pl.program_id(0)
    ff = up.shape[2]

    @pl.when(step == 0)
    def _():
        for k in range(many):
            w[k, :, ff:] = router[...]
        grt[...] = jnp.zeros_like(grt)

    for k in range(many):
        for i in range(n):
            xs[k, i * per * cap : (i + 1) * per * cap, :] = xs_in[i][k]
            gs[k, i * per * cap : (i + 1) * per * cap, :] = gs_in[i][k]
        w[k, :, :ff] = up[k]
    both = [jnp.dot(xs[k], w[k], preferred_element_type=F32) for k in range(many)]
    us = [jnp.dot(gs[k], down[k], preferred_element_type=F32) for k in range(many)]
    scaled = []
    for k in range(many):
        pre, u = both[k][:, :ff], us[k]
        sel = lax.broadcasted_iota(jnp.int32, pre.shape, 1) == step * many + k
        logit = jnp.sum(jnp.where(sel, both[k][:, ff:], 0.0), axis=1, keepdims=True)
        chosen = jax.nn.sigmoid(logit)
        square = pre * pre
        t = jnp.tanh(GELU_C * (pre + GELU_K * (square * pre)))
        half = 0.5 * (1.0 + t)
        act = (half * pre).astype(BF)
        slope = half + 0.5 * pre * (1.0 - t * t) * (GELU_C * (1.0 + 3.0 * GELU_K * square))
        act32 = act.astype(F32)
        dchosen = jnp.sum(u * act32, axis=1, keepdims=True)
        drl = dchosen * chosen * (1.0 - chosen)
        scaled.append((chosen * act32).astype(BF))
        d2[k, :, :ff] = (chosen * u * slope).astype(BF)
        d2[k, :, ff:] = jnp.where(sel, drl, 0.0).astype(BF)
    for k in range(many):
        dgot = lax.dot_general(
            d2[k], w[k], (((1,), (1,)), ((), ())), preferred_element_type=F32
        ).astype(BF)
        got = lax.dot_general(
            scaled[k], down[k], (((1,), (1,)), ((), ())), preferred_element_type=F32
        ).astype(BF)
        for s in range(groups):
            moe[s][k] = got[s * cap : (s + 1) * cap]
            dhid[s][k] = dgot[s * cap : (s + 1) * cap]
    x_size, _, _, _, lanes = near.shape
    for k in range(many):
        gu = lax.dot_general(d2[k], xs[k], (((0,), (0,)), ((), ())), preferred_element_type=F32)
        gacc[k, 0] = gu[:ff]
        grt[...] += gu[ff : ff + grt.shape[0]]
        gacc[k, 1] = lax.dot_general(
            scaled[k], gs[k], (((0,), (0,)), ((), ())), preferred_element_type=F32
        )
        for xr in range(x_size):
            base = lax.rem(at_ref[1] + xr, x_size) * 2
            for cr, out in enumerate((near, far)):
                cut = pl.multiple_of((base + lax.rem(at_ref[0] + cr, 2)) * lanes, lanes)
                for i in range(2):
                    out[xr, k, i] = gacc[k, i, :, pl.ds(cut, lanes)].astype(BF)


def expert_call(coords, x_size, groups, xs, gs, up, down, router, cap, many=2):
    n = len(xs)
    experts, width, ff = up.shape
    per = groups // n
    rows = groups * cap
    pad = -(-experts // 8) * 8
    lanes = width // (2 * x_size)
    row_spec = pl.BlockSpec((many, per * cap, width), lambda e, _: (e, 0, 0))
    w_spec = pl.BlockSpec((many, width, ff), lambda e, _: (e, 0, 0))
    whole = lambda *shape: pl.BlockSpec(shape, lambda e, _: (0,) * len(shape))
    g_spec = pl.BlockSpec((x_size, many, 2, ff, lanes), lambda e, _: (0, e, 0, 0, 0))
    s_spec = pl.BlockSpec((many, cap, width), lambda e, _: (e, 0, 0))
    one = jax.ShapeDtypeStruct((experts, cap, width), BF)
    outs = pl.pallas_call(
        functools.partial(expert_kernel, groups, per, cap, many),
        grid_spec=pltpu.PrefetchScalarGridSpec(
            num_scalar_prefetch=1,
            grid=(experts // many,),
            in_specs=[row_spec] * (2 * n) + [w_spec, w_spec, whole(width, ff)],
            out_specs=[s_spec] * (2 * groups) + [g_spec, g_spec, whole(pad, width)],
            scratch_shapes=[
                pltpu.VMEM((many, rows, width), BF),
                pltpu.VMEM((many, rows, width), BF),
                pltpu.VMEM((many, width, 2 * ff), BF),
                pltpu.VMEM((many, rows, 2 * ff), BF),
                pltpu.VMEM((many, 2, ff, width), F32),
            ],
        ),
        out_shape=[one] * (2 * groups)
        + [jax.ShapeDtypeStruct((x_size, experts, 2, ff, lanes), BF)] * 2
        + [jax.ShapeDtypeStruct((pad, width), F32)],
        compiler_params=pltpu.CompilerParams(vmem_limit_bytes=VMEM_LIMIT),
        cost_estimate=pl.CostEstimate(
            flops=experts * rows * width * ff * 2 * 8,
            bytes_accessed=experts * rows * width * 8,
            transcendentals=0,
        ),
        name="experts",
    )(coords, *xs, *gs, up, down, router)
    return outs[:groups], outs[groups : 2 * groups], outs[-3], outs[-2], outs[-1]


def scatter_kernel(js, *refs):
    count = len(js)
    rows, slots, outs = refs[:count], [refs[count].at[j] for j in js], refs[count + 1 :]
    experts, cap, width = rows[0].shape
    all_slots = experts * cap
    rowi = lax.broadcasted_iota(jnp.int32, (experts, all_slots), 0)
    coli = lax.broadcasted_iota(jnp.int32, (experts, all_slots), 1)
    spread = (coli // cap == rowi).astype(F32).astype(BF)
    for s in range(count):
        wide = jnp.dot(slots[s][...], spread, preferred_element_type=F32)
        lane = lax.broadcasted_iota(jnp.int32, wide.shape, 1) % cap
        put = (wide == lane.astype(F32)).astype(F32).astype(BF)
        outs[s][...] = jnp.dot(
            put, rows[s][...].reshape(all_slots, width), preferred_element_type=F32
        ).astype(BF)


def scatter_call(rows, slots, js):
    count = len(rows)
    experts, cap, width = rows[0].shape
    seq_rows = slots.shape[1]
    return pl.pallas_call(
        functools.partial(scatter_kernel, js),
        out_shape=[jax.ShapeDtypeStruct((seq_rows, width), BF)] * count,
        compiler_params=pltpu.CompilerParams(vmem_limit_bytes=40 * 1024 * 1024),
        cost_estimate=pl.CostEstimate(
            flops=2 * count * seq_rows * experts * cap * width,
            bytes_accessed=2 * count * experts * cap * width,
            transcendentals=0,
        ),
        name="scatter_rows",
    )(*rows, slots)


AXES = ("x", "lo", "hi")


def spread_kernel(sizes, first, rows, at_ref, *refs):
    left, left_far, right, right_far = refs[:4]
    turned, res = refs[-2:]
    outs = refs[-2 - sizes[first] : -2]
    extra = refs[4] if len(refs) == 4 + len(outs) + 3 else None
    seq_rows = left.shape[0]
    x_size, lo, hi = sizes

    @pl.when(pl.program_id(0) == 0)
    def _():
        turned[:, :seq_rows] = jnp.transpose(left[...])
        turned[:, seq_rows:] = jnp.transpose(left_far[...])

    got = jnp.dot(turned[:, :seq_rows], right[...], preferred_element_type=F32)
    got += jnp.dot(turned[:, seq_rows:], right_far[...], preferred_element_type=F32)
    res[...] = got if extra is None else got + extra[...].astype(F32)
    for xr in range(x_size):
        x = lax.rem(at_ref[1] + xr, x_size)
        for lr in range(lo):
            l = lax.rem(at_ref[2] + lr, lo)
            for hr in range(hi):
                h = lax.rem(at_ref[3] + hr, hi)
                start = pl.multiple_of(((x * hi + h) * lo + l) * rows, rows)
                place = [xr, lr, hr]
                out = outs[place.pop(first)]
                out[place[0], place[1]] = res[pl.ds(start, rows), :].astype(BF)


def spread_call(coords, grid, left, right, tile, first, extra=None):
    seq_rows, width = left[0].shape
    cols = right[0].shape[1]
    sizes = (grid.xs, grid.lo, grid.hi)
    at = AXES.index(first)
    others = sizes[:at] + sizes[at + 1 :]
    rows = width // math.prod(sizes)
    o_spec = pl.BlockSpec((*others, rows, tile), lambda j, _: (0, 0, 0, j))
    in_specs = [pl.BlockSpec((seq_rows, width), lambda j, _: (0, 0))] * 2
    in_specs += [pl.BlockSpec((seq_rows, tile), lambda j, _: (0, j))] * 2
    args = [*left, *right]
    if extra is not None:
        in_specs.append(pl.BlockSpec((width, tile), lambda j, _: (0, j)))
        args.append(extra)
    return pl.pallas_call(
        functools.partial(spread_kernel, sizes, at, rows),
        grid_spec=pltpu.PrefetchScalarGridSpec(
            num_scalar_prefetch=1,
            grid=(cols // tile,),
            in_specs=in_specs,
            out_specs=[o_spec] * sizes[at],
            scratch_shapes=[pltpu.VMEM((width, 2 * seq_rows), BF), pltpu.VMEM((width, tile), F32)],
        ),
        out_shape=[jax.ShapeDtypeStruct((*others, rows, cols), BF)] * sizes[at],
        compiler_params=pltpu.CompilerParams(vmem_limit_bytes=40 * 1024 * 1024),
        cost_estimate=pl.CostEstimate(
            flops=4 * seq_rows * width * cols, bytes_accessed=2 * width * cols, transcendentals=0
        ),
        name="weight_grad",
    )(coords, *args)


NT = (((1,), (1,)), ((), ()))
TN = (((0,), (0,)), ((), ()))


def dot_nt(a, b):
    return lax.dot_general(a, b, NT, preferred_element_type=F32)


def dot_tn(a, b):
    return lax.dot_general(a, b, TN, preferred_element_type=F32)


def dot(a, b):
    return jnp.dot(a, b, preferred_element_type=F32)


def column(x, at):
    lane = lax.broadcasted_iota(jnp.int32, x.shape, 1)
    return jnp.sum(jnp.where(lane == at, x, 0.0), axis=1, keepdims=True)


def pick_mask(choice):
    picks = choice.shape[1]
    row = lax.broadcasted_iota(jnp.int32, (picks, HEADS * AEXP), 0)
    head = lax.broadcasted_iota(jnp.int32, (picks, HEADS * AEXP), 1) // AEXP
    low = choice.astype(F32).astype(BF)
    first = dot(low, (row == 2 * head).astype(F32).astype(BF))
    second = dot(low, (row == 2 * head + 1).astype(F32).astype(BF))
    expert = (lax.broadcasted_iota(jnp.int32, first.shape, 1) % AEXP).astype(F32)
    return ((first == expert) | (second == expert)).astype(F32)


def normalize(x):
    mean = jnp.mean(x, axis=1, keepdims=True)
    centered = x - mean
    inverse = lax.rsqrt(jnp.mean(centered * centered, axis=1, keepdims=True) + 1e-05)
    return centered * inverse, inverse


def probabilities(q, k, length):
    scores = dot_nt(q, k) * (1.0 / math.sqrt(HEAD))
    row = lax.broadcasted_iota(jnp.int32, scores.shape, 0)
    col = lax.broadcasted_iota(jnp.int32, scores.shape, 1)
    scores = jnp.where((col <= row) & (col < length), scores, -1e30)
    expo = jnp.exp(scores - jnp.max(scores, axis=1, keepdims=True))
    return expo / jnp.sum(expo, axis=1, keepdims=True)


def forward_kernel(
    length_ref, tokens, gain, cos, sin, wq, wk, wv, wo, vr, orr, vc, oc,
    hidden, hidden_low, normed, q_out, k_out, mixed_out, vals_out, att_out, exp_out,
    vsig, vmask, osig, omask, acc,
):
    h = pl.program_id(0)

    @pl.when(h == 0)
    def _():
        scaled, _ = normalize(tokens[...].astype(F32))
        normed[...] = (scaled * gain[...]).astype(BF)
        vsig[...] = jax.nn.sigmoid(dot(tokens[...], vr[...]))
        osig[...] = jax.nn.sigmoid(dot(tokens[...], orr[...]))
        vmask[...] = pick_mask(vc[...])
        omask[...] = pick_mask(oc[...])
        acc[...] = tokens[...].astype(F32)

    q = dot(normed[...], wq[...])
    k = dot(normed[...], wk[...])
    q = (q * cos[...] + pltpu.roll(q, HEAD // 2, 1) * sin[...]).astype(BF)
    k = (k * cos[...] + pltpu.roll(k, HEAD // 2, 1) * sin[...]).astype(BF)
    q_out[...] = q
    k_out[...] = k
    vals = dot(tokens[...], wv[...])
    vals_out[...] = vals
    gate = vsig[...] * vmask[...]
    mixed = jnp.zeros_like(q, F32)
    for e in range(AEXP):
        mixed += column(gate, h * AEXP + e) * vals[:, e * HEAD : (e + 1) * HEAD]
    mixed = mixed.astype(BF)
    mixed_out[...] = mixed
    probs = probabilities(q, k, length_ref[0]).astype(BF)
    att = dot(probs, mixed)
    att_out[...] = att
    gate = osig[...] * omask[...]
    for e in range(AEXP):
        exp_out[:, e * HEAD : (e + 1) * HEAD] = (column(gate, h * AEXP + e) * att).astype(BF)
    acc[...] += dot_nt(exp_out[...], wo[...])

    @pl.when(h == pl.num_programs(0) - 1)
    def _():
        hidden[...] = acc[...]
        hidden_low[...] = acc[...].astype(BF)


def whole_spec(*shape):
    return pl.BlockSpec(shape, lambda h, _: (0,) * len(shape))


def head_spec(rows, cols):
    return pl.BlockSpec((rows, cols), lambda h, _: (0, h))


def forward_call(lengths, tokens, gain, cos, sin, wq, wk, wv, wo, vr, orr, vc, oc):
    rows, width = tokens.shape
    many = AEXP * HEAD
    gates = HEADS * AEXP
    shape = lambda cols, kind: jax.ShapeDtypeStruct((rows, cols), kind)
    return pl.pallas_call(
        forward_kernel,
        grid_spec=pltpu.PrefetchScalarGridSpec(
            num_scalar_prefetch=1,
            grid=(HEADS,),
            in_specs=[
                whole_spec(rows, width),
                whole_spec(1, width),
                whole_spec(rows, HEAD),
                whole_spec(rows, HEAD),
                head_spec(width, HEAD),
                head_spec(width, HEAD),
                head_spec(width, many),
                head_spec(width, many),
                whole_spec(width, gates),
                whole_spec(width, gates),
                whole_spec(rows, 2 * HEADS),
                whole_spec(rows, 2 * HEADS),
            ],
            out_specs=[
                whole_spec(rows, width),
                whole_spec(rows, width),
                whole_spec(rows, width),
                head_spec(rows, HEAD),
                head_spec(rows, HEAD),
                head_spec(rows, HEAD),
                head_spec(rows, many),
                head_spec(rows, HEAD),
                head_spec(rows, many),
            ]
            + [whole_spec(rows, gates)] * 4,
            scratch_shapes=[pltpu.VMEM((rows, width), F32)],
        ),
        out_shape=[
            shape(width, F32),
            shape(width, BF),
            shape(width, BF),
            shape(HEADS * HEAD, BF),
            shape(HEADS * HEAD, BF),
            shape(HEADS * HEAD, BF),
            shape(HEADS * many, F32),
            shape(HEADS * HEAD, F32),
            shape(HEADS * many, BF),
        ]
        + [shape(gates, F32)] * 4,
        compiler_params=pltpu.CompilerParams(vmem_limit_bytes=40 * 1024 * 1024),
        cost_estimate=pl.CostEstimate(
            flops=2 * rows * width * HEADS * (2 * HEAD + 2 * many),
            bytes_accessed=2 * width * HEADS * (2 * HEAD + 2 * many),
            transcendentals=0,
        ),
        name="attention_forward",
    )(lengths, tokens, gain, cos, sin, wq, wk, wv, wo, vr, orr, vc, oc)


def backward_kernel(
    length_ref, dbranch, cos, sin, wo, q_in, k_in, mixed_in, vals, att, vsig, vmask, osig, omask,
    dqk, dvals, dlogits, dl,
):
    h = pl.program_id(0)

    @pl.when(h == 0)
    def _():
        dl[...] = jnp.zeros_like(dl)

    lane = lax.broadcasted_iota(jnp.int32, dl.shape, 1)
    scale = 1.0 / math.sqrt(HEAD)
    dexp = dot(dbranch[...], wo[...])
    datt = jnp.zeros_like(att)
    for e in range(AEXP):
        at = h * AEXP + e
        part = dexp[:, e * HEAD : (e + 1) * HEAD]
        sig, mask = column(osig[...], at), column(omask[...], at)
        datt += (sig * mask) * part
        logit = jnp.sum(part * att[...], axis=1, keepdims=True) * mask * sig * (1.0 - sig)
        dl[...] += jnp.where(lane == HEADS * AEXP + at, logit, 0.0)
    datt = datt.astype(BF)
    q, k, mixed = q_in[...], k_in[...], mixed_in[...]
    probs = probabilities(q, k, length_ref[0])
    dp = dot_nt(datt, mixed)
    inner = jnp.sum(probs * dp, axis=1, keepdims=True)
    dscore = (probs * (dp - inner)).astype(BF)
    dq = dot(dscore, k) * scale
    dk = dot_tn(dscore, q) * scale
    dmixed = dot_tn(probs.astype(BF), datt)
    dqk[:, :HEAD] = (dq * cos[...] - pltpu.roll(dq, HEAD // 2, 1) * sin[...]).astype(BF)
    dqk[:, HEAD:] = (dk * cos[...] - pltpu.roll(dk, HEAD // 2, 1) * sin[...]).astype(BF)
    for e in range(AEXP):
        at = h * AEXP + e
        part = vals[:, e * HEAD : (e + 1) * HEAD]
        sig, mask = column(vsig[...], at), column(vmask[...], at)
        dvals[:, e * HEAD : (e + 1) * HEAD] = ((sig * mask) * dmixed).astype(BF)
        logit = jnp.sum(part * dmixed, axis=1, keepdims=True) * mask * sig * (1.0 - sig)
        dl[...] += jnp.where(lane == at, logit, 0.0)

    @pl.when(h == pl.num_programs(0) - 1)
    def _():
        dlogits[...] = dl[...].astype(BF)


def backward_call(lengths, dbranch, cos, sin, wo, q, k, mixed, vals, att, gates):
    rows, width = dbranch.shape
    many = AEXP * HEAD
    return pl.pallas_call(
        backward_kernel,
        grid_spec=pltpu.PrefetchScalarGridSpec(
            num_scalar_prefetch=1,
            grid=(HEADS,),
            in_specs=[
                whole_spec(rows, width),
                whole_spec(rows, HEAD),
                whole_spec(rows, HEAD),
                head_spec(width, many),
                head_spec(rows, HEAD),
                head_spec(rows, HEAD),
                head_spec(rows, HEAD),
                head_spec(rows, many),
                head_spec(rows, HEAD),
            ]
            + [whole_spec(rows, HEADS * AEXP)] * 4,
            out_specs=[head_spec(rows, 2 * HEAD), head_spec(rows, many), whole_spec(rows, 128)],
            scratch_shapes=[pltpu.VMEM((rows, 128), F32)],
        ),
        out_shape=[
            jax.ShapeDtypeStruct((rows, HEADS * 2 * HEAD), BF),
            jax.ShapeDtypeStruct((rows, HEADS * many), BF),
            jax.ShapeDtypeStruct((rows, 128), BF),
        ],
        compiler_params=pltpu.CompilerParams(vmem_limit_bytes=40 * 1024 * 1024),
        cost_estimate=pl.CostEstimate(
            flops=2 * rows * width * HEADS * many * 2,
            bytes_accessed=2 * width * HEADS * many,
            transcendentals=0,
        ),
        name="attention_backward",
    )(lengths, dbranch, cos, sin, wo, q, k, mixed, vals, att, *gates)


def input_kernel(tokens, gain, dhidden, dqk, dvals, dlogits, wq, wk, wv, vr, orr, out, dn, rest):
    h = pl.program_id(0)

    @pl.when(h == 0)
    def _():
        gates = HEADS * AEXP
        dn[...] = jnp.zeros_like(dn)
        rest[...] = (
            dhidden[...]
            + dot_nt(dlogits[:, :gates], vr[...])
            + dot_nt(dlogits[:, gates : 2 * gates], orr[...])
        )

    dn[...] += dot_nt(dqk[:, :HEAD], wq[...]) + dot_nt(dqk[:, HEAD:], wk[...])
    rest[...] += dot_nt(dvals[...], wv[...])

    @pl.when(h == pl.num_programs(0) - 1)
    def _():
        scaled, inverse = normalize(tokens[...].astype(F32))
        dscaled = dn[...] * gain[...]
        inside = (
            dscaled
            - jnp.mean(dscaled, axis=1, keepdims=True)
            - scaled * jnp.mean(dscaled * scaled, axis=1, keepdims=True)
        )
        out[...] = (rest[...] + inverse * inside).astype(BF)


def input_call(tokens, gain, dhidden, dqk, dvals, dlogits, wq, wk, wv, vr, orr):
    rows, width = tokens.shape
    many = AEXP * HEAD
    whole = lambda *shape: pl.BlockSpec(shape, lambda h: (0,) * len(shape))
    head = lambda *shape: pl.BlockSpec(shape, lambda h: (0, h))
    return pl.pallas_call(
        input_kernel,
        grid=(HEADS,),
        in_specs=[
            whole(rows, width),
            whole(1, width),
            whole(rows, width),
            head(rows, 2 * HEAD),
            head(rows, many),
            whole(rows, 128),
            head(width, HEAD),
            head(width, HEAD),
            head(width, many),
            whole(width, HEADS * AEXP),
            whole(width, HEADS * AEXP),
        ],
        out_specs=whole(rows, width),
        out_shape=jax.ShapeDtypeStruct((rows, width), BF),
        scratch_shapes=[pltpu.VMEM((rows, width), F32)] * 2,
        compiler_params=pltpu.CompilerParams(vmem_limit_bytes=40 * 1024 * 1024),
        cost_estimate=pl.CostEstimate(
            flops=2 * rows * width * HEADS * (many + 2 * HEAD),
            bytes_accessed=2 * width * HEADS * (many + 2 * HEAD),
            transcendentals=0,
        ),
        name="input_grad",
    )(tokens, gain, dhidden, dqk, dvals, dlogits, wq, wk, wv, vr, orr)


def shards(
    tokens,
    norm_gain,
    query_weight,
    key_weight,
    value_weight,
    output_weight,
    value_router,
    output_router,
    expert_router,
    expert_up,
    expert_down,
    lengths,
    value_choice,
    output_choice,
    expert_choice,
    running_counts,
    cotangent,
):
    seq_rows, model_width = tokens.shape
    groups = lax.axis_size("expert")
    grid = Grid(lax.axis_size("dp"), groups)
    coords = grid.coords()
    me = lax.axis_index("expert")
    local_experts, _, ff = expert_up.shape
    experts_all = local_experts * groups
    picks_per = expert_choice.shape[1]
    cap = 3 * seq_rows * picks_per // (2 * experts_all)
    position = jnp.arange(seq_rows, dtype=jnp.int32)
    seq_length = lengths[0]

    code = jnp.where((position < seq_length)[:, None], expert_choice + 1, 0)
    all_grads, all_codes, all_hidden = {}, {}, {}
    grad_ring = Task(grid.gather_rows(cotangent, all_grads, True))
    code_ring = Task(grid.gather_rows(jnp.transpose(code), all_codes))

    cosine, sine = rope_tables(seq_rows, HEAD)
    gain = norm_gain.reshape(1, model_width)
    vc = value_choice.reshape(seq_rows, -1)
    oc = output_choice.reshape(seq_rows, -1)
    core = coords[0]

    def split(x, axis=1):
        return grid.half(x, axis, core), grid.core_shift(grid.half(x, axis, 1 - core))

    if grid.lo == 2:
        end_round([grad_ring, code_ring])
    forward = forward_call(
        lengths, tokens, gain, cosine, sine, query_weight, key_weight, value_weight, output_weight,
        value_router, output_router, vc, oc,
    )
    forward = end_round([grad_ring, code_ring], forward)
    hidden, hidden_low, normed_low, query_rot, key_rot, mixed, values_all, attended, expanded = (
        forward[:9]
    )
    gates = forward[9:]
    tokens_both, normed_both, expanded_far, hidden_low = end_round(
        [grad_ring, code_ring],
        (split(tokens), split(normed_low), grid.core_shift(expanded), hidden_low),
    )

    ring = Task(grid.gather_rows(hidden_low, all_hidden))
    end_round([ring, code_ring])
    finish([code_ring])
    codes = [all_codes[j] for j in range(groups)]
    slot, slot_low = slot_call(codes, (me * local_experts).reshape(1), local_experts)

    def take(known, j):
        return gather_call([known[j], known[j + 1]], slot, (j, j + 1), cap)

    xs, gs = {}, {}
    if grid.lo == 2:
        gs[0], gs[2] = end_round([ring], (take(all_grads, 0), take(all_grads, 2)))
        gs[4], xs[0] = end_round([ring, grad_ring], (take(all_grads, 4), take(all_hidden, 0)))
        xs[2], xs[4] = end_round([ring, grad_ring], (take(all_hidden, 2), take(all_hidden, 4)))
    finish([ring, grad_ring])
    for j in range(0, groups, 2):
        xs[j] = xs[j] if j in xs else take(all_hidden, j)
        gs[j] = gs[j] if j in gs else take(all_grads, j)
    xs = [xs[j] for j in range(0, groups, 2)]
    gs = [gs[j] for j in range(0, groups, 2)]

    router_mine = lax.dynamic_slice_in_dim(expert_router, me * local_experts, local_experts, 1)
    router_pad = jnp.pad(router_mine, ((0, 0), (0, ff - local_experts)))
    moe_rows, dhid_rows, near, far, grad_router_t = expert_call(
        coords, grid.xs, groups, xs, gs, expert_up, expert_down, router_pad, cap
    )
    dhid, moe = {}, {}

    def scatter(rows, known, places):
        js = [grid.at(*place) for place in places]
        for j, value in zip(js, scatter_call([rows[j] for j in js], slot_low, js)):
            known[j] = value
        return [known[j] for j in js]

    def home(rows, known):
        def part(j):
            if j not in known:
                mate = j ^ 1
                got = scatter_call([rows[j], rows[mate]], slot_low, (j, mate))
                known[j], known[mate] = got
            return known[j]

        return part

    devices = grid.dp * groups
    rows_each = model_width // devices
    labels_all = jnp.arange(experts_all, dtype=jnp.int32)
    local_counts = jnp.sum(
        (code[:, :, None] == labels_all + 1).astype(jnp.int32), axis=(0, 1), dtype=jnp.int32
    )
    bits = (local_counts[:, None] >> jnp.arange(6, dtype=jnp.int32)) & 1
    bits = bits.reshape(devices, experts_all // devices, 6)
    bits = jnp.pad(bits, ((0, 0), (0, rows_each - experts_all // devices), (0, 0)))
    bits = bits.reshape(model_width, 6).astype(BF)
    routers = 2 * HEADS * AEXP
    small = -(-(routers + experts_all + 6) // 256) * 256
    extra = jnp.pad(bits, ((0, 0), (routers + experts_all, small - routers - experts_all - 6)))
    extra = lax.dynamic_update_slice_in_dim(
        extra,
        jnp.transpose(grad_router_t)[:, :local_experts].astype(BF),
        routers + me * local_experts,
        1,
    )
    extra_near, extra_far = split(extra, 0)

    two = grid.lo == 2
    if two:
        scatter(dhid_rows, dhid, [(3, 1), (0, 1)])
    back = Task(grid.sum_rows_hi(home(dhid_rows, dhid)))
    shares = Task(grid.expert_tree(near, far, 4))
    if two:
        end_round([back, shares], scatter(dhid_rows, dhid, [(2, 1), (3, 0)]))
        _, extra_far = end_round([back, shares], (scatter(dhid_rows, dhid, [(2, 0), (1, 1)]), extra_far))
        end_round(
            [back, shares],
            scatter(dhid_rows, dhid, [(1, 0), (0, 0)]) + scatter(moe_rows, moe, [(3, 1), (3, 0)]),
        )
    extra = add(extra_near, extra_far)
    out_ring = Task(grid.sum_rows(home(moe_rows, moe)))
    more = scatter(moe_rows, moe, [(2, 1), (2, 0)]) if two else ()
    _, extra = end_round([back, shares, out_ring], (more, extra))
    finish([back])
    dhidden = total(cotangent, *back.result)
    dbranch_low = dhidden.astype(BF)

    dbranch_both = split(dbranch_low)
    own = backward_call(
        lengths, dbranch_low, cosine, sine, output_weight, query_rot, key_rot, mixed, values_all,
        attended, gates,
    )
    more = scatter(moe_rows, moe, [(1, 1), (1, 0)]) if two else ()
    own, dbranch_both, _ = end_round([out_ring, shares], (own, dbranch_both, more))
    other = [grid.core_shift(v) for v in own]
    output_parts = spread_call(coords, grid, dbranch_both, (expanded, expanded_far), 512, "x")
    more = scatter(moe_rows, moe, [(0, 1), (0, 0)]) if two else ()
    own, other, output_parts, _ = end_round([out_ring, shares], (own, other, output_parts, more))
    finish([shares])
    output_sum = Task(grid.tree(output_parts, ("x", "lo", "hi")))
    dqk, dvalues, dlogits = zip(own, other)
    cut = dvalues[0].shape[1] // 2
    value_parts = [
        spread_call(coords, grid, tokens_both, [v[:, c : c + cut] for v in dvalues], 640, "lo")
        for c in (0, cut)
    ]
    qk_part = spread_call(coords, grid, normed_both, dqk, 512, "hi")
    wide = [jnp.pad(v, ((0, 0), (0, small - v.shape[1]))) for v in dlogits]
    small_part = spread_call(coords, grid, tokens_both, wide, small, "hi", extra)
    value_parts, qk_part, small_part = end_round([out_ring], (value_parts, qk_part, small_part))
    finish([out_ring])

    first_sum = Task(grid.tree(value_parts[0], ("lo", "x", "hi")))
    second_sum = Task(grid.tree(value_parts[1], ("lo", "x", "hi")))
    qk_sum = Task(grid.tree(qk_part, ("hi", "x", "lo")))
    small_sum = Task(grid.tree(small_part, ("hi", "x", "lo")))
    grad_tokens = input_call(
        tokens, gain, dhidden, own[0], own[1], own[2], query_weight, key_weight,
        value_weight, value_router, output_router,
    )
    grad_tokens = end_round([output_sum, first_sum, qk_sum, small_sum], grad_tokens)
    expert_grads = jnp.concatenate([total(*parts) for parts in shares.result], axis=0)
    expert_grads = [jnp.swapaxes(expert_grads[:, i], 1, 2) for i in range(2)]
    expert_grads = end_round([first_sum, second_sum, qk_sum, small_sum], expert_grads)
    output = (hidden + total(*out_ring.result)).astype(BF)
    output = end_round([output_sum, first_sum, second_sum, qk_sum, small_sum], output)
    finish([output_sum, first_sum, second_sum, qk_sum, small_sum])
    sum_output, sum_qk, sum_small = output_sum.result, qk_sum.result, small_sum.result
    sum_value = jnp.concatenate([first_sum.result, second_sum.result], axis=1)
    qk = HEADS * HEAD
    sum_qk = jnp.swapaxes(sum_qk.reshape(rows_each, HEADS, 2, HEAD), 1, 2)
    grad_query = sum_qk[:, 0].reshape(rows_each, qk)
    grad_key = sum_qk[:, 1].reshape(rows_each, qk)
    first = (lax.axis_index("dp") * groups + me) * rows_each
    rows_of = lambda w: lax.dynamic_slice_in_dim(w, first, rows_each, 0)
    grad_gain = jnp.sum(
        grad_query * rows_of(query_weight).astype(F32) + grad_key * rows_of(key_weight).astype(F32),
        axis=1,
    ) / rows_of(norm_gain)
    half = HEADS * AEXP
    got_bits = sum_small[: experts_all // devices, routers + experts_all :][:, :6]
    got_counts = jnp.sum(got_bits * (2.0 ** jnp.arange(6, dtype=F32)), axis=1)
    counts = running_counts + got_counts.astype(jnp.int32)
    return (
        output,
        grad_tokens,
        grad_gain,
        grad_query,
        grad_key,
        sum_value,
        sum_output,
        sum_small[:, :half],
        sum_small[:, half:routers],
        sum_small[:, routers : routers + experts_all],
        *expert_grads,
        counts,
    )


def solution(mesh):
    both = ("dp", "expert")
    in_specs = (
        P(both, None),
        P(),
        P(),
        P(),
        P(),
        P(),
        P(),
        P(),
        P(),
        P("expert", None, None),
        P("expert", None, None),
        P(both),
        P(both, None, None),
        P(both, None, None),
        P(both, None),
        P(both),
        P(both, None),
    )
    out_specs = (
        P(both, None),
        P(both, None),
        P(both),
        P(both, None),
        P(both, None),
        P(both, None),
        P(both, None),
        P(both, None),
        P(both, None),
        P(both, None),
        P("expert", "dp", None),
        P("expert", "dp", None),
        P(both),
    )
    return jax.shard_map(shards, mesh=mesh, in_specs=in_specs, out_specs=out_specs, check_vma=False)
```

time: 531 us -> 426 us (0.80)
  waiting for transfers between devices: 251 us -> 76.8 us
  Pallas kernels: 75.5 us -> 123 us
  matrix products: 45.2 us -> 0 us
  local copies, waits for them, and re-layouts: 48.2 us -> 85 us
  starting transfers between devices: 41.7 us -> 75.2 us
    ppermute x20 -> x23, waiting for transfers between devices: 125 us -> 29.5 us  [lo_shift(): return lax.ppermute(x, 'expert', pairs)]
    ppermute x5 -> x9, waiting for transfers between devices: 83.5 us -> 7.91 us  [x_shift(): return lax.ppermute(x, 'dp', pairs)]
    pallas_call x13 -> x26, Pallas kernels: 75.5 us -> 123 us  [the longest x1 34.1 us: expert_call(): pl.pallas_call(functools.partial(expert_kernel, groups, per, cap, many),...]
    dot_general x18 -> x0, matrix products: 42.4 us -> none  [the longest x6 17.5 us: contract_cols(): lax.dot_general(left, right, (((1,), (1,)), ((), ())), preferred_element_...]
    unnamed x174 -> x235, local copies, waits for them, and re-layouts: 26.5 us -> 54.6 us
    ppermute x24 -> x32, starting transfers between devices: 8.83 us -> 35 us  [hi_shift(): return lax.ppermute(x, 'expert', pairs)]
    add x5 -> x9, other arithmetic: 1.55 us -> 15.7 us  [total(): return functools.reduce(lambda a, b: a + b, [p.astype(F32) for p in parts])]
    dynamic_slice x0 -> x4, local copies, waits for them, and re-layouts: none -> 13.3 us  [half(): x = lax.dynamic_index_in_dim(x, core, axis + 1, False)]
  transfers between devices with their start and end apart: 54 -> 73, of which waited for: 35 -> 24; matrix products, arithmetic and copies ran while one was open for 22% -> 23% of each run, Pallas kernels for 2% -> 19%
where the time goes in v2:
time: 426 us; the launch traced here: 420 us
  Pallas kernels  123 us (29%)
  local copies, waits for them, and re-layouts  85 us (20%)
  waiting for transfers between devices  76.8 us (18%)
  starting transfers between devices  75.2 us (18%)
  other arithmetic  56.7 us (13%)
    unnamed x235, local copies, waits for them, and re-layouts  54.6 us
    ppermute x32, waiting for transfers between devices, hi_shift(): return lax.ppermute(x, 'expert', pairs)  39.4 us
    ppermute x32, starting transfers between devices, hi_shift(): return lax.ppermute(x, 'expert', pairs)  35 us
    pallas_call x1, Pallas kernels, expert_call(): pl.pallas_call(functools.partial(expert_kernel, groups, per, cap, many),...  34.1 us
    pallas_call x8, Pallas kernels, gather_call(): pl.pallas_call(functools.partial(gather_kernel, js, cap), grid=(experts /...  32.8 us
    ppermute x23, waiting for transfers between devices, lo_shift(): return lax.ppermute(x, 'expert', pairs)  29.5 us
    convert_element_type x25, other arithmetic, add(): return total(*parts).astype(BF)  29.1 us
    ppermute x23, starting transfers between devices, lo_shift(): return lax.ppermute(x, 'expert', pairs)  28.9 us
  transfers between devices with their start and end apart: 73, of which 24 were waited for; matrix products, arithmetic and copies ran while one was open for 23% of the time, Pallas kernels for 19%

profile of v2, /device:TPU:0, one launch (start us, length us, event | category | flops | bytes accessed | tf_op | source)
XLA Modules:
  0.0 420.2 jit_solution(2685707712697816201)
XLA Ops:
  9.3 6.9 %collective-permute-done.2.refs_1_ = s32[16,256]{1,0:T(8,128)S(1)} collective-permute-done((s32[16,256]{1,0:T(8,128)S(1)}, s32[16,256]{1,0:T(8,128)S(1)}, u32[]{:S(2)}, u32[]{:S(2)}) %collective-permute-start.2) | collective-permute-done | bytes 16416 | tf_op jit(solution)/shard_map/ppermute | solution.py:105
  29.4 11.1 %attention_forward.1 = (f32[256,1024]{1,0:T(8,128)S(1)}, bf16[256,1024]{1,0:T(8,128)(2,1)S(1)}, bf16[256,1024]{1,0:T(8,128)(2,1)S(1)}, bf16[256,512]{1,0:T(8,128...) custom-call(s32[1]{0:T(128)} %copy.105.length_ref, ...), custom_call_target="tpu_custom_call" | custom-call | flops 3221225472 | bytes 12582912 | tf_op jit(solution)/shard_map/attention_forward/pallas_call | solution.py:590
  53.3 5.5 %dynamic-slice_reduce_fusion.2 = (bf16[256,2,256]{2,1,0:T(2,128)(2,1)S(1)}, bf16[256,2,256]{2,1,0:T(2,128)(2,1)}) fusion(bf16[256,2,2,256]{3,2,1,0:T(2,128)(2,1)} %reshape.312, s32[]{:T(128)S(6)} %select_n.53, s32[]{:T(128)S(6)} %select_n.52), kind=kLoop, calls=%fused_computation.37 | loop fusion | bytes 1048584 | tf_op jit(solution)/shard_map/jit(dynamic_index_in_dim)/dynamic_slice | solution.py:85
  60.7 4.9 %dynamic-slice_reduce_fusion = (bf16[256,2,256]{2,1,0:T(2,128)(2,1)S(1)}, bf16[256,2,256]{2,1,0:T(2,128)(2,1)S(1)}) fusion(bf16[256,2,2,256]{3,2,1,0:T(2,128)(2,1)} %reshape.315, s32[]{:T(128)S(6)} %select_n.53, s32[]{:T(128)S(6)} %select_n.52), kind=kLoop, calls=%fused_computation.35 | loop fusion | bytes 1048584 | tf_op jit(solution)/shard_map/jit(dynamic_index_in_dim)/dynamic_slice | solution.py:85
  79.0 9.6 %collective-permute-done.17.refs_7_ = s32[16,256]{1,0:T(8,128)S(1)} collective-permute-done((s32[16,256]{1,0:T(8,128)S(1)}, s32[16,256]{1,0:T(8,128)S(1)}, u32[]{:S(2)}, u32[]{:S(2)}) %collective-permute-start.17) | collective-permute-done | bytes 16416 | tf_op jit(solution)/shard_map/ppermute | solution.py:105
  93.9 4.1 gather_rows.9.refs_5_
  98.0 4.2 gather_rows.8.refs_4_
  105.4 4.1 gather_rows.11.refs_0_
  109.5 4.1 gather_rows.10.refs_6_
  113.6 4.0 collective-permute-done.21.refs_0_
  119.4 4.1 gather_rows.12.refs_1_
  123.4 4.1 gather_rows.13.refs_2_
  129.0 4.1 gather_rows.15.refs_7_
  133.1 4.1 gather_rows.14.refs_3_
  137.3 34.1 %experts.1 = (bf16[24,32,1024]{2,1,0:T(8,128)(2,1)}, bf16[24,32,1024]{2,1,0:T(8,128)(2,1)}, bf16[24,32,1024]{2,1,0:T(8,128)(2,1)}, bf16[24,32,1024]{2,1,0:T(8,12...) custom-call(s32[4]{0:T(128)} %pad_add_fusion.at_ref, ...), custom_call_target="tpu_custom_call" | custom-call | flops 12884901888 | bytes 50331648 | tf_op jit(solution)/shard_map/experts/pallas_call | solution.py:358
  186.2 6.9 %collective-permute-done.26 = bf16[256,1024]{1,0:T(8,128)(2,1)} collective-permute-done((bf16[256,1024]{1,0:T(8,128)(2,1)}, bf16[256,1024]{1,0:T(8,128)(2,1)}, u32[]{:S(2)}, u32[]{:S(2)}) %collective-permute-start.26) | collective-permute-done | bytes 524320 | tf_op jit(solution)/shard_map/ppermute | solution.py:99
  201.4 3.8 dynamic_update_slice.3
  225.2 8.2 %collective-permute-done.33 = bf16[256,1024]{1,0:T(8,128)(2,1)S(1)} collective-permute-done((bf16[256,1024]{1,0:T(8,128)(2,1)S(1)}, bf16[256,1024]{1,0:T(8,128)(2,1)S(1)}, u32[]{:S(2)}, u32[]{:S(2)}) %collective-permute-start.33) | collective-permute-done | bytes 524320 | tf_op jit(solution)/shard_map/ppermute | solution.py:99
  284.2 10.1 %attention_backward.1 = (bf16[256,1024]{1,0:T(8,128)(2,1)}, bf16[256,2560]{1,0:T(8,128)(2,1)S(1)}, bf16[256,128]{1,0:T(8,128)(2,1)S(1)}) custom-call(s32[1]{0:T(128)} %copy.105.length_ref, bf16[256,1024]{1,0:T(8,128)(2,1)S(1)} %get-tuple-element.455.dbranch, f32[256,128]{1,0:T(8,128)S(1)} %get-tuple-element.491.cos, f32[256,128]{1,0:T(8,128)S(1)} %copy-done.32, ...), custom_call_target="tpu_custom_call" | custom-call | flops 2684354560 | bytes 5242880 | tf_op jit(solution)/shard_map/attention_backward/pallas_call | solution.py:693
  309.1 5.6 %weight_grad.5 = (bf16[2,4,32,2560]{3,2,1,0:T(8,128)(2,1)S(1)}, bf16[2,4,32,2560]{3,2,1,0:T(8,128)(2,1)S(1)}) custom-call(s32[4]{0:T(128)S(1)} %copy-done.77, bf16[256,512]{1,0:T(8,128)(2,1)S(1)} %copy.80.refs_0_, bf16[256,512]{1,0:T(8,128)(2,1)} %collective-permute-done.41.refs_1_, bf16[256,2560]{1,0:T(8,128)(2,1)} %get-tuple-element.228.refs_2_, ...), custom_call_target="tpu_custom_call" | custom-call | flops 1342177280 | bytes 2621440 | tf_op jit(solution)/shard_map/weight_grad/pallas_call | solution.py:466
  329.2 5.5 %collective-permute-done.48 = bf16[256,1024]{1,0:T(8,128)(2,1)S(1)} collective-permute-done((bf16[256,1024]{1,0:T(8,128)(2,1)S(1)}, bf16[256,1024]{1,0:T(8,128)(2,1)S(1)}, u32[]{:S(2)}, u32[]{:S(2)}) %collective-permute-start.48) | collective-permute-done | bytes 524320 | tf_op jit(solution)/shard_map/ppermute | solution.py:99
  342.8 6.8 %input_grad.1 = bf16[256,1024]{1,0:T(8,128)(2,1)} custom-call(bf16[256,1024]{1,0:T(8,128)(2,1)S(1)} %copy-done.4, f32[1,1024]{1,0:T(1,128)S(1)} %bitcast.209, f32[256,1024]{1,0:T(8,128)S(1)} %copy-done.8, bf16[256,1024]{1,0:T(8,128)(2,1)} %get-tuple-element.344.refs_2_.dqk, bf16[256,2560]{1,0:T(8,128)(2,1)S(1)} %get-tuple-element.336.dvals, ...), custom_call_target="tpu_custom_call" | custom-call | flops 1879048192 | bytes 7340032 | tf_op jit(solution)/shard_map/input_grad/pallas_call | solution.py:761
  361.3 5.9 %collective-permute-done.54 = bf16[2,4,32,1280]{3,2,1,0:T(8,128)(2,1)S(1)} collective-permute-done((bf16[2,4,32,1280]{3,2,1,0:T(8,128)(2,1)S(1)}, bf16[2,4,32,1280]{3,2,1,0:T(8,128)(2,1)S(1)}, u32[]{:S(2)}, u32[]{:S(2)}) %collective-permute-start.54) | collective-permute-done | bytes 655392 | tf_op jit(solution)/shard_map/ppermute | solution.py:105
  370.4 4.0 collective-permute-start.57
  (467 shorter events, 251.4 us)
Async XLA Ops:
  0.7 19.0 %collective-permute-start = (bf16[256,1024]{1,0:T(8,128)(2,1)}, bf16[256,1024]{1,0:T(8,128)(2,1)S(1)}, u32[]{:S(2)}, u32[]{:S(2)}) collective-permute-start(bf16[256,1024]{1,0:T(8,128)(2,1)} %refs_0_.1), channel_id=1, source_target_pairs={{0,1},{1,0},{2,3},{3,2},{4,5},{5,4},{6,7},{7,6},{8,9},{9,8},{10,11... | collective-permute-start | bytes 1572872 | tf_op jit(solution)/shard_map/ppermute | solution.py:105
  19.7 29.7 %collective-permute-start.4 = (bf16[256,1024]{1,0:T(8,128)(2,1)}, bf16[256,1024]{1,0:T(8,128)(2,1)}, u32[]{:S(2)}, u32[]{:S(2)}) collective-permute-start(bf16[256,1024]{1,0:T(8,128)(2,1)} %collective-permute-done.1.refs_0_), channel_id=1, source_target_pairs={{0,1},{1,0},{2,3},{3,2},{4,5},{5,4},{6,7},{7,6},{8,9},{9,8},{10,11... | collective-permute-start | bytes 1572872 | tf_op jit(solution)/shard_map/ppermute | solution.py:105
  20.2 29.1 %collective-permute-start.5 = (bf16[256,1024]{1,0:T(8,128)(2,1)}, bf16[256,1024]{1,0:T(8,128)(2,1)}, u32[]{:S(2)}, u32[]{:S(2)}) collective-permute-start(bf16[256,1024]{1,0:T(8,128)(2,1)} %collective-permute-done.1.refs_0_), channel_id=1, source_target_pairs={{0,2},{1,3},{2,4},{3,5},{4,6},{5,7},{6,0},{7,1},{8,10},{9,11},{10,... | collective-permute-start | bytes 1572872 | tf_op jit(solution)/shard_map/ppermute | solution.py:99
  24.9 23.9 %collective-permute-start.6 = (s32[16,256]{1,0:T(8,128)}, s32[16,256]{1,0:T(8,128)S(1)}, u32[]{:S(2)}, u32[]{:S(2)}) collective-permute-start(s32[16,256]{1,0:T(8,128)} %collective-permute-done.3.refs_2_), channel_id=1, source_target_pairs={{0,1},{1,0},{2,3},{3,2},{4,5},{5,4},{6,7},{7,6},{8,9},{9,8},{10,11... | collective-permute-start | bytes 49160 | tf_op jit(solution)/shard_map/ppermute | solution.py:105
  26.2 23.1 %collective-permute-start.7 = (s32[16,256]{1,0:T(8,128)}, s32[16,256]{1,0:T(8,128)}, u32[]{:S(2)}, u32[]{:S(2)}) collective-permute-start(s32[16,256]{1,0:T(8,128)} %collective-permute-done.3.refs_2_), channel_id=1, source_target_pairs={{0,2},{1,3},{2,4},{3,5},{4,6},{5,7},{6,0},{7,1},{8,10},{9,11},{10,... | collective-permute-start | bytes 49160 | tf_op jit(solution)/shard_map/ppermute | solution.py:99
  49.4 27.2 %collective-permute-start.14 = (bf16[256,2560]{1,0:T(8,128)(2,1)}, bf16[256,2560]{1,0:T(8,128)(2,1)}, u32[]{:S(2)}, u32[]{:S(2)}) collective-permute-start(bf16[256,2560]{1,0:T(8,128)(2,1)} %get-tuple-element.228.refs_2_), channel_id=1, source_target_pairs={{0,8},{8,0},{16,24},{24,16},{1,9},{9,1},{17,25},{25,17},{2,10},{10... | collective-permute-start | bytes 3932168 | tf_op jit(solution)/shard_map/ppermute | solution.py:89
  49.4 27.2 %collective-permute-start.8 = (bf16[256,1024]{1,0:T(8,128)(2,1)}, bf16[256,1024]{1,0:T(8,128)(2,1)}, u32[]{:S(2)}, u32[]{:S(2)}) collective-permute-start(bf16[256,1024]{1,0:T(8,128)(2,1)} %collective-permute-done.5.refs_0_), channel_id=1, source_target_pairs={{0,1},{1,0},{2,3},{3,2},{4,5},{5,4},{6,7},{7,6},{8,9},{9,8},{10,11... | collective-permute-start | bytes 1572872 | tf_op jit(solution)/shard_map/ppermute | solution.py:105
  50.0 26.6 %collective-permute-start.9 = (bf16[256,1024]{1,0:T(8,128)(2,1)}, bf16[256,1024]{1,0:T(8,128)(2,1)}, u32[]{:S(2)}, u32[]{:S(2)}) collective-permute-start(bf16[256,1024]{1,0:T(8,128)(2,1)} %collective-permute-done.5.refs_0_), channel_id=1, source_target_pairs={{0,2},{1,3},{2,4},{3,5},{4,6},{5,7},{6,0},{7,1},{8,10},{9,11},{10,... | collective-permute-start | bytes 1572872 | tf_op jit(solution)/shard_map/ppermute | solution.py:99
  171.4 21.8 %collective-permute-start.28 = (bf16[2,24,2,128,256]{4,3,2,1,0:T(8,128)(2,1)}, bf16[2,24,2,128,256]{4,3,2,1,0:T(8,128)(2,1)}, u32[]{:S(2)}, u32[]{:S(2)}) collective-permute-start(bf16[2,24,2,128,256]{4,3,2,1,0:T(8,128)(2,1)} %get-tuple-element.280), channel_id=1, source_target_pairs={{0,8},{8,0},{16,24},{24,16},{1,9},{9,1},{17,25},{25,17},{2,10},{10... | collective-permute-start | bytes 18874376 | tf_op jit(solution)/shard_map/ppermute | solution.py:89
  184.8 25.7 %collective-permute-start.30 = (bf16[256,1024]{1,0:T(8,128)(2,1)}, bf16[256,1024]{1,0:T(8,128)(2,1)}, u32[]{:S(2)}, u32[]{:S(2)}) collective-permute-start(bf16[256,1024]{1,0:T(8,128)(2,1)} %get-tuple-element.281), channel_id=1, source_target_pairs={{0,2},{1,3},{2,4},{3,5},{4,6},{5,7},{6,0},{7,1},{8,10},{9,11},{10,... | collective-permute-start | bytes 1572872 | tf_op jit(solution)/shard_map/ppermute | solution.py:99
  195.7 19.0 %collective-permute-start.31 = (bf16[6,2,128,256]{3,2,1,0:T(8,128)(2,1)}, bf16[6,2,128,256]{3,2,1,0:T(8,128)(2,1)}, u32[]{:S(2)}, u32[]{:S(2)}) collective-permute-start(bf16[6,2,128,256]{3,2,1,0:T(8,128)(2,1)} %fusion), channel_id=1, source_target_pairs={{0,16},{8,24},{16,0},{24,8},{1,17},{9,25},{17,1},{25,9},{2,18},{10... | collective-permute-start | bytes 2359304 | tf_op jit(solution)/shard_map/ppermute | solution.py:93
  216.4 17.8 %collective-permute-start.35 = (bf16[6,2,128,256]{3,2,1,0:T(8,128)(2,1)S(1)}, bf16[6,2,128,256]{3,2,1,0:T(8,128)(2,1)S(1)}, u32[]{:S(2)}, u32[]{:S(2)}) collective-permute-start(bf16[6,2,128,256]{3,2,1,0:T(8,128)(2,1)S(1)} %fusion.1), channel_id=1, source_target_pairs={{0,16},{8,24},{16,0},{24,8},{1,17},{9,25},{17,1},{25,9},{2,18},{10... | collective-permute-start | bytes 2359304 | tf_op jit(solution)/shard_map/ppermute | solution.py:93
  221.5 30.4 %collective-permute-start.38 = (bf16[256,1024]{1,0:T(8,128)(2,1)}, bf16[256,1024]{1,0:T(8,128)(2,1)}, u32[]{:S(2)}, u32[]{:S(2)}) collective-permute-start(bf16[256,1024]{1,0:T(8,128)(2,1)} %get-tuple-element.292), channel_id=1, source_target_pairs={{0,1},{1,0},{2,3},{3,2},{4,5},{5,4},{6,7},{7,6},{8,9},{9,8},{10,11... | collective-permute-start | bytes 1572872 | tf_op jit(solution)/shard_map/ppermute | solution.py:105
  237.0 17.3 %collective-permute-start.37 = (bf16[6,2,128,256]{3,2,1,0:T(8,128)(2,1)}, bf16[6,2,128,256]{3,2,1,0:T(8,128)(2,1)}, u32[]{:S(2)}, u32[]{:S(2)}) collective-permute-start(bf16[6,2,128,256]{3,2,1,0:T(8,128)(2,1)} %fusion.2), channel_id=1, source_target_pairs={{0,16},{8,24},{16,0},{24,8},{1,17},{9,25},{17,1},{25,9},{2,18},{10... | collective-permute-start | bytes 2359304 | tf_op jit(solution)/shard_map/ppermute | solution.py:93
  244.2 50.1 %collective-permute-start.25 = (bf16[256,1024]{1,0:T(8,128)(2,1)}, bf16[256,1024]{1,0:T(8,128)(2,1)}, u32[]{:S(2)}, u32[]{:S(2)}) collective-permute-start(bf16[256,1024]{1,0:T(8,128)(2,1)} %get-tuple-element.263), channel_id=1, source_target_pairs={{0,1},{1,0},{2,3},{3,2},{4,5},{5,4},{6,7},{7,6},{8,9},{9,8},{10,11... | collective-permute-start | bytes 1572872 | tf_op jit(solution)/shard_map/ppermute | solution.py:105
  248.9 65.9 %collective-permute-start.24 = (bf16[256,1024]{1,0:T(8,128)(2,1)}, bf16[256,1024]{1,0:T(8,128)(2,1)}, u32[]{:S(2)}, u32[]{:S(2)}) collective-permute-start(bf16[256,1024]{1,0:T(8,128)(2,1)} %get-tuple-element.259), channel_id=1, source_target_pairs={{0,1},{1,0},{2,3},{3,2},{4,5},{5,4},{6,7},{7,6},{8,9},{9,8},{10,11... | collective-permute-start | bytes 1572872 | tf_op jit(solution)/shard_map/ppermute | solution.py:105
  261.2 33.1 %collective-permute-start.41 = (bf16[256,512]{1,0:T(8,128)(2,1)}, bf16[256,512]{1,0:T(8,128)(2,1)}, u32[]{:S(2)}, u32[]{:S(2)}) collective-permute-start(bf16[256,512]{1,0:T(8,128)(2,1)} %copy.79), channel_id=1, source_target_pairs={{0,8},{8,0},{16,24},{24,16},{1,9},{9,1},{17,25},{25,17},{2,10},{10... | collective-permute-start | bytes 786440 | tf_op jit(solution)/shard_map/ppermute | solution.py:89
  263.7 30.7 %collective-permute-start.40 = (bf16[6,2,128,256]{3,2,1,0:T(8,128)(2,1)}, bf16[6,2,128,256]{3,2,1,0:T(8,128)(2,1)}, u32[]{:S(2)}, u32[]{:S(2)}) collective-permute-start(bf16[6,2,128,256]{3,2,1,0:T(8,128)(2,1)} %fusion.3), channel_id=1, source_target_pairs={{0,16},{8,24},{16,0},{24,8},{1,17},{9,25},{17,1},{25,9},{2,18},{10... | collective-permute-start | bytes 2359304 | tf_op jit(solution)/shard_map/ppermute | solution.py:93
  267.2 27.1 %collective-permute-start.39 = (bf16[256,1024]{1,0:T(8,128)(2,1)}, bf16[256,1024]{1,0:T(8,128)(2,1)}, u32[]{:S(2)}, u32[]{:S(2)}) collective-permute-start(bf16[256,1024]{1,0:T(8,128)(2,1)} %add_convert_fusion.9), channel_id=1, source_target_pairs={{0,2},{1,3},{2,4},{3,5},{4,6},{5,7},{6,0},{7,1},{8,10},{9,11},{10,... | collective-permute-start | bytes 1572872 | tf_op jit(solution)/shard_map/ppermute | solution.py:99
  294.3 21.9 %collective-permute-start.44 = (bf16[256,2560]{1,0:T(8,128)(2,1)S(1)}, bf16[256,2560]{1,0:T(8,128)(2,1)}, u32[]{:S(2)}, u32[]{:S(2)}) collective-permute-start(bf16[256,2560]{1,0:T(8,128)(2,1)S(1)} %get-tuple-element.336.dvals), channel_id=1, source_target_pairs={{0,8},{8,0},{16,24},{24,16},{1,9},{9,1},{17,25},{25,17},{2,10},{10... | collective-permute-start | bytes 3932168 | tf_op jit(solution)/shard_map/ppermute | solution.py:89
  319.9 32.1 %collective-permute-start.46 = (bf16[2,4,32,2560]{3,2,1,0:T(8,128)(2,1)S(1)}, bf16[2,4,32,2560]{3,2,1,0:T(8,128)(2,1)}, u32[]{:S(2)}, u32[]{:S(2)}) collective-permute-start(bf16[2,4,32,2560]{3,2,1,0:T(8,128)(2,1)S(1)} %get-tuple-element.331), channel_id=1, source_target_pairs={{0,16},{8,24},{16,0},{24,8},{1,17},{9,25},{17,1},{25,9},{2,18},{10... | collective-permute-start | bytes 3932168 | tf_op jit(solution)/shard_map/ppermute | solution.py:93
  349.6 17.7 %collective-permute-start.54 = (bf16[2,4,32,1280]{3,2,1,0:T(8,128)(2,1)S(1)}, bf16[2,4,32,1280]{3,2,1,0:T(8,128)(2,1)S(1)}, u32[]{:S(2)}, u32[]{:S(2)}) collective-permute-start(bf16[2,4,32,1280]{3,2,1,0:T(8,128)(2,1)S(1)} %get-tuple-element.363), channel_id=1, source_target_pairs={{0,1},{1,0},{2,3},{3,2},{4,5},{5,4},{6,7},{7,6},{8,9},{9,8},{10,11... | collective-permute-start | bytes 1966088 | tf_op jit(solution)/shard_map/ppermute | solution.py:105
  359.3 28.1 %collective-permute-start.52 = (bf16[4,32,2560]{2,1,0:T(8,128)(2,1)}, bf16[4,32,2560]{2,1,0:T(8,128)(2,1)}, u32[]{:S(2)}, u32[]{:S(2)}) collective-permute-start(bf16[4,32,2560]{2,1,0:T(8,128)(2,1)} %get-tuple-element.460), channel_id=1, source_target_pairs={{0,1},{1,0},{2,3},{3,2},{4,5},{5,4},{6,7},{7,6},{8,9},{9,8},{10,11... | collective-permute-start | bytes 1966088 | tf_op jit(solution)/shard_map/ppermute | solution.py:105
  369.1 18.2 %collective-permute-start.60 = (bf16[4,32,1280]{2,1,0:T(8,128)(2,1)}, bf16[4,32,1280]{2,1,0:T(8,128)(2,1)S(1)}, u32[]{:S(2)}, u32[]{:S(2)}) collective-permute-start(bf16[4,32,1280]{2,1,0:T(8,128)(2,1)} %get-tuple-element.462), channel_id=1, source_target_pairs={{0,16},{8,24},{16,0},{24,8},{1,17},{9,25},{17,1},{25,9},{2,18},{10... | collective-permute-start | bytes 983048 | tf_op jit(solution)/shard_map/ppermute | solution.py:93
  (160 other events, 1364.9 us)
